TPU v7x, 256 devices: a whole 4x4x8 slice. The times are simulated.
256 devices in a mesh: pat: 8 (over x, core), slab: 32 (over y, z).
Axes of the slice: x: 4, y: 4, z: 8, core: 2. Of those that a mesh axis runs over, the one named last changes fastest.
Arguments:
- features: bfloat16 [8, 64, 192, 384], P('pat', None, 'slab'), may hold values from -50 to 50
- cotangent: bfloat16 [8, 64, 192, 384], P('pat', None, 'slab'), may hold values from -50 to 50
- weights: float32 [2, 64, 1728], replicated, may hold values from -0.15625 to 0.15625
- prev_state: float32 [2, 64, 1728], replicated, may hold values from -6 to 6
- tree_noise: float32 [2, 64, 1728], replicated, may hold values from -6 to 6
Outputs:
- state_next: float32 [2, 64, 1728], replicated
- weights_next: float32 [2, 64, 1728], replicated
All inputs are finite; a program needn't handle non-finite values.
Results may differ from a plain program's by a relative error of at most 0.006.
Values may be sent and summed in bfloat16 or wider, within the bound.
A program may use at most 64 MiB of HBM per device.

v0:
```python
import jax
import jax.numpy as jnp
from jax import lax
from jax.sharding import PartitionSpec as P

W = 24


eps_norm = 1e-05
clip_bound = 400.0
step_rate = 0.1


def padded_2(shard, sides, width):
    for axis, dim in sides:
        peers, length = (lax.axis_size(axis), shard.shape[dim])
        up = [(i, (i + 1) % peers) for i in range(peers - 1)]
        down = [(j, i) for i, j in up]
        last = lax.slice_in_dim(shard, length - width, length, axis=dim)
        initial = lax.slice_in_dim(shard, 0, width, axis=dim)
        before = lax.ppermute(last, axis, up)
        after = lax.ppermute(initial, axis, down)
        shard = jnp.concatenate([before, shard, after], axis=dim)
    return shard


def depth_rims(volume, width):
    return padded_2(volume, (("slab", 1),), width)


def slab_totals(first, second):
    return lax.psum((first, second), "slab")


def plane_taps(volume):
    plane_size = volume.shape[2]
    padded = jnp.pad(volume, ((0, 0), (0, 0), (W + 1, W + 1)))
    column = lax.broadcasted_iota(jnp.int32, (1, 1, plane_size), 2) % W
    pieces = []
    for row_step in (-1, 0, 1):
        for col_step in (-1, 0, 1):
            offset = W + 1 + row_step * W + col_step
            shifted = padded[:, :, offset : offset + plane_size]
            if col_step != 0:
                inside = (column + col_step >= 0) & (column + col_step < W)
                shifted = jnp.where(inside, shifted, jnp.zeros_like(shifted))
            pieces.append(shifted)
    return jnp.concatenate(pieces, axis=0)


def convolve(padded_field, kernel):
    channels = kernel.shape[0]
    planes = padded_field.shape[1] - 2
    summed = None
    for depth_step in range(3):
        stacked = plane_taps(padded_field[:, depth_step : depth_step + planes, :])
        block_cols = kernel[:, depth_step * 9 * channels : (depth_step + 1) * 9 * channels]
        partial_value = jnp.einsum(
            "oi,izp->ozp", block_cols, stacked, preferred_element_type=jnp.float32
        )
        summed = partial_value if summed is None else summed + partial_value
    return summed


def kernel_grad(padded_field, upstream):
    planes = upstream.shape[1]
    blocks = []
    for depth_step in range(3):
        stacked = plane_taps(padded_field[:, depth_step : depth_step + planes, :])
        blocks.append(
            jnp.einsum("ozp,izp->oi", upstream, stacked, preferred_element_type=jnp.float32)
        )
    return jnp.concatenate(blocks, axis=1)


def flipped(kernel):
    channels = kernel.shape[0]
    return jnp.flip(kernel.reshape(channels, 27, channels).transpose(2, 1, 0), axis=1).reshape(
        channels, 27 * channels
    )


def statistics(summed, cell_count):
    totals, squares = slab_totals(
        jnp.sum(summed, axis=(1, 2)), jnp.sum(summed * summed, axis=(1, 2))
    )
    centre = totals / cell_count
    spread = lax.rsqrt(squares / cell_count - centre * centre + eps_norm)
    return (centre[:, None, None], spread[:, None, None])


def norm_back(gradient, normed, spread, cell_count):
    totals, crossed = slab_totals(
        jnp.sum(gradient, axis=(1, 2)), jnp.sum(gradient * normed, axis=(1, 2))
    )
    return spread * (
        gradient
        - (totals / cell_count)[:, None, None]
        - normed * (crossed / cell_count)[:, None, None]
    )


def silu_slope(values):
    sigmoid_val = jax.nn.sigmoid(values)
    return sigmoid_val * (1.0 + values * (1.0 - sigmoid_val))


def per_device(features, cotangent, weights, prev_state, tree_noise):
    kernels = weights.astype(jnp.bfloat16)
    conv_one = kernels[0]
    conv_two = kernels[1]
    volume = features[0]
    upstream = cotangent[0]
    planes = volume.shape[1]
    cell_count = lax.axis_size("slab") * planes * volume.shape[2]
    input_rims = depth_rims(volume, 1)
    first = convolve(input_rims, conv_one)
    centre_one, spread_one = statistics(first, cell_count)
    normed_one = (first - centre_one) * spread_one
    hidden = jax.nn.silu(normed_one).astype(jnp.bfloat16)
    hidden_rims = depth_rims(hidden, 1)
    second = convolve(hidden_rims, conv_two)
    centre_two, spread_two = statistics(second, cell_count)
    normed_two = (second - centre_two) * spread_two
    gradient_two = upstream.astype(jnp.float32) * silu_slope(normed_two)
    cotan_two = norm_back(gradient_two, normed_two, spread_two, cell_count).astype(jnp.bfloat16)
    kgrad_two = kernel_grad(hidden_rims, cotan_two)
    back_hidden = convolve(depth_rims(cotan_two, 1), flipped(conv_two))
    gradient_one = back_hidden * silu_slope(normed_one)
    cotan_one = norm_back(gradient_one, normed_one, spread_one, cell_count).astype(jnp.bfloat16)
    kgrad_one = kernel_grad(input_rims, cotan_one)
    sum_one, sum_two = lax.psum((kgrad_one, kgrad_two), "slab")
    squared = jnp.sum(sum_one * sum_one) + jnp.sum(sum_two * sum_two)
    factor = clip_bound / jnp.maximum(jnp.sqrt(squared), clip_bound)
    total_one, total_two = lax.psum((factor * sum_one, factor * sum_two), "pat")
    combined = jnp.stack([total_one, total_two])
    state_next = prev_state + combined
    weights_next = weights - step_rate * (combined + tree_noise)
    return (state_next, weights_next)


def solution(mesh):
    return jax.shard_map(
        per_device,
        mesh=mesh,
        in_specs=(P("pat", None, "slab", None), P("pat", None, "slab", None), P(), P(), P()),
        out_specs=(P(), P()),
        check_vma=False,
    )
```

profile of v0, /device:TPU:1, one launch (start us, length us, event | category | flops | bytes accessed | tf_op | source)
XLA Modules:
  0.0 595.0 jit_solution(10123902198371959285)
XLA Ops:
  9.4 5.0 collective-permute-start
  27.7 1.5 fusion.158
  29.2 62.4 %all-reduce.12 = (f32[64]{0:T(128)S(1)}, f32[64]{0:T(128)S(1)}) all-reduce(f32[64]{0:T(128)S(1)} %get-tuple-element.9, f32[64]{0:T(128)S(1)} %get-tuple-element.8), channel_id=1, replica_groups=mesh['pat'=8,'slab'=32] {'slab'}, use_global_device_ids=true, to_apply=%region_1.2 | all-reduce | flops 128 | bytes 1024 | tf_op jit(solution)/shard_map/psum | solution.py:32
  93.2 4.2 collective-permute-start.2
  105.9 57.8 %all-reduce.11 = (f32[64]{0:T(128)S(1)}, f32[64]{0:T(128)S(1)}) all-reduce(f32[64]{0:T(128)S(1)} %get-tuple-element.7, f32[64]{0:T(128)S(1)} %get-tuple-element.6), channel_id=1, replica_groups=mesh['pat'=8,'slab'=32] {'slab'}, use_global_device_ids=true, to_apply=%region_5.6 | all-reduce | flops 128 | bytes 1024 | tf_op jit(solution)/shard_map/psum | solution.py:32
  163.7 2.4 fusion.156
  166.1 55.7 %all-reduce.10 = (f32[64]{0:T(128)S(1)}, f32[64]{0:T(128)S(1)}) all-reduce(f32[64]{0:T(128)S(1)} %get-tuple-element.5, f32[64]{0:T(128)S(1)} %get-tuple-element.4), channel_id=1, replica_groups=mesh['pat'=8,'slab'=32] {'slab'}, use_global_device_ids=true, to_apply=%region_11.12 | all-reduce | flops 128 | bytes 1024 | tf_op jit(solution)/shard_map/psum | solution.py:32
  221.9 1.7 fusion.10
  223.6 3.5 convolution_bitcast_fusion
  227.1 1.6 convolution_bitcast_fusion.1
  228.7 1.6 convolution_bitcast_fusion.2
  232.2 4.6 collective-permute-start.4
  237.7 2.0 concatenate.76
  239.6 1.7 pad_maximum_fusion
  246.7 1.5 fusion.155
  248.2 56.8 %all-reduce.9 = (f32[64]{0:T(128)S(1)}, f32[64]{0:T(128)S(1)}) all-reduce(f32[64]{0:T(128)S(1)} %get-tuple-element.3, f32[64]{0:T(128)S(1)} %get-tuple-element.2), channel_id=1, replica_groups=mesh['pat'=8,'slab'=32] {'slab'}, use_global_device_ids=true, to_apply=%region_15.16 | all-reduce | flops 128 | bytes 1024 | tf_op jit(solution)/shard_map/psum | solution.py:32
  305.0 1.5 fusion.20
  306.5 2.7 convolution_bitcast_fusion.3
  311.9 197.1 %all-reduce.18.cloned.1.call-done = (f32[64,1728]{1,0:T(8,128)}, f32[64,1728]{1,0:T(8,128)}) async-done(((f32[64,1728]{1,0:T(8,128)}, f32[64,1728]{1,0:T(8,128)}), (f32[64,1728]{1,0:T(8,128)}, f32[64,1728]{1,0:T(8,128)})) %all-reduce.18.cloned.1.call-update) | async-done | bytes 884752 | tf_op jit(solution)/shard_map/psum | solution.py:132
  509.1 1.9 multiply_reduce_fusion.2
  511.0 1.7 multiply_reduce_fusion.3
  514.1 1.8 multiply_bitcast_fusion
  515.9 1.8 multiply_bitcast_fusion.1
  517.7 66.8 %all-reduce.20.cloned.1.call-done = (f32[1,64,1728]{2,1,0:T(8,128)}, f32[1,64,1728]{2,1,0:T(8,128)}) async-done(((f32[1,64,1728]{2,1,0:T(8,128)}, f32[1,64,1728]{2,1,0:T(8,128)}), (f32[1,64,1728]{2,1,0:T(8,128)}, f32[1,64,1728]{2,1,0:T(8,128)})) %all-reduce.20.cloned.1.call-update) | async-done | bytes 884752 | tf_op jit(solution)/shard_map/psum | solution.py:135
  (141 shorter events, 39.5 us)
Async XLA Ops:
  7.2 8.5 %copy-start = (bf16[1,64,6,384]{3,1,2,0:T(8,128)(2,1)S(1)}, bf16[1,64,6,384]{3,1,2,0:T(8,128)(2,1)}, u32[]{:S(2)}) copy-start(bf16[1,64,6,384]{3,1,2,0:T(8,128)(2,1)} %param.5) | copy-start | bytes 884740
  7.2 501.9 %all-reduce.18.cloned.1.call-start = ((), (), s32[]{:S(2)}) async-start(), calls=%async_computation | async-start | bytes 1835008 | tf_op jit(solution)/shard_map/psum | solution.py:132
  8.1 12.6 %collective-permute-start.1 = (bf16[64,1,384]{2,0,1:T(8,128)(2,1)S(1)}, bf16[64,1,384]{2,0,1:T(8,128)(2,1)S(1)}, u32[]{:S(2)}, u32[]{:S(2)}) collective-permute-start(bf16[64,1,384]{2,0,1:T(8,128)(2,1)S(1)} %get-tuple-element.41), channel_id=1, source_target_pairs={{1,0},{2,1},{3,2},{4,3},{5,4},{6,5},{7,6},{8,7},{9,8},{10,9},{11,1... | collective-permute-start | bytes 147464 | tf_op jit(solution)/shard_map/ppermute | solution.py:22
  9.4 11.3 %collective-permute-start = (bf16[64,1,384]{2,0,1:T(8,128)(2,1)S(1)}, bf16[64,1,384]{2,0,1:T(8,128)(2,1)S(1)}, u32[]{:S(2)}, u32[]{:S(2)}) collective-permute-start(bf16[64,1,384]{2,0,1:T(8,128)(2,1)S(1)} %get-tuple-element.42), channel_id=1, source_target_pairs={{0,1},{1,2},{2,3},{3,4},{4,5},{5,6},{6,7},{7,8},{8,9},{9,10},{10,1... | collective-permute-start | bytes 147464 | tf_op jit(solution)/shard_map/ppermute | solution.py:21
  15.7 10.4 %copy-start.12 = (bf16[64,1728]{1,0:T(8,128)(2,1)}, bf16[64,1728]{1,0:T(8,128)(2,1)S(1)}, u32[]{:S(2)}) copy-start(bf16[64,1728]{1,0:T(8,128)(2,1)S(1)} %get-tuple-element.27) | copy-start | bytes 663556
  21.6 1.7 copy-start.5
  24.6 3.1 copy-start.8
  91.9 5.6 collective-permute-start.3
  93.2 5.2 collective-permute-start.2
  100.6 3.9 copy-start.9
  102.1 1.6 copy-start.3
  102.6 1.8 copy-start.1
  163.7 58.2 %copy-start.16 = (f32[64]{0:T(128)}, f32[64]{0:T(128)S(1)}, u32[]{:S(2)}) copy-start(f32[64]{0:T(128)S(1)} %get-tuple-element.53) | copy-start | bytes 772
  163.7 58.2 %copy-start.17 = (f32[64]{0:T(128)}, f32[64]{0:T(128)S(1)}, u32[]{:S(2)}) copy-start(f32[64]{0:T(128)S(1)} %get-tuple-element.52) | copy-start | bytes 772
  221.8 5.2 copy-start.4
  223.6 5.1 copy-start.2
  230.9 8.7 %collective-permute-start.5 = (bf16[64,1,384]{2,0,1:T(8,128)(2,1)}, bf16[64,1,384]{2,0,1:T(8,128)(2,1)}, u32[]{:S(2)}, u32[]{:S(2)}) collective-permute-start(bf16[64,1,384]{2,0,1:T(8,128)(2,1)} %get-tuple-element.31), channel_id=1, source_target_pairs={{1,0},{2,1},{3,2},{4,3},{5,4},{6,5},{7,6},{8,7},{9,8},{10,9},{11,1... | collective-permute-start | bytes 147464 | tf_op jit(solution)/shard_map/ppermute | solution.py:22
  232.2 7.4 %collective-permute-start.4 = (bf16[64,1,384]{2,0,1:T(8,128)(2,1)}, bf16[64,1,384]{2,0,1:T(8,128)(2,1)}, u32[]{:S(2)}, u32[]{:S(2)}) collective-permute-start(bf16[64,1,384]{2,0,1:T(8,128)(2,1)} %get-tuple-element.32), channel_id=1, source_target_pairs={{0,1},{1,2},{2,3},{3,4},{4,5},{5,6},{6,7},{7,8},{8,9},{9,10},{10,1... | collective-permute-start | bytes 147464 | tf_op jit(solution)/shard_map/ppermute | solution.py:21
  241.5 1.8 copy-start.11
  305.0 4.2 copy-start.7
  311.9 272.6 %all-reduce.20.cloned.1.call-start = ((), (), s32[]{:S(2)}) async-start(), calls=%async_computation.1 | async-start | bytes 1835008 | tf_op jit(solution)/shard_map/psum | solution.py:135
  509.1 77.5 %copy-start.10 = (f32[2,64,1728]{2,1,0:T(8,128)S(1)}, f32[2,64,1728]{2,1,0:T(8,128)}, u32[]{:S(2)}) copy-start(f32[2,64,1728]{2,1,0:T(8,128)} %param.7) | copy-start | bytes 2654212
  509.1 77.6 %copy-start.13 = (f32[2,64,1728]{2,1,0:T(8,128)S(1)}, f32[2,64,1728]{2,1,0:T(8,128)}, u32[]{:S(2)}) copy-start(f32[2,64,1728]{2,1,0:T(8,128)} %param.9) | copy-start | bytes 2654212
  509.1 77.6 %copy-start.14 = (f32[2,64,1728]{2,1,0:T(8,128)S(1)}, f32[2,64,1728]{2,1,0:T(8,128)}, u32[]{:S(2)}) copy-start(f32[2,64,1728]{2,1,0:T(8,128)} %param.8) | copy-start | bytes 2654212
  (2 other events, 2.9 us)
Sparse Core Ops, SparseCore 0:
  312.0 197.0 all-reduce.17
  517.9 66.5 all-reduce.19
where the time goes:
time: 597 us; the launch traced here: 595 us
  waiting for transfers between devices  265 us (44%)
  blocking collectives  233 us (39%)
  other arithmetic  28.8 us (5%)
  matrix products  18.9 us (3%)
  starting transfers between devices  17.7 us (3%)
  between operations  16.2 us (3%)
  local copies, waits for them, and re-layouts  15.9 us (3%)
    psum x4, blocking collectives, slab_totals(): return lax.psum((first, second), 'slab')  233 us
    psum x1, waiting for transfers between devices, per_device(): sum_one, sum_two = lax.psum((kgrad_one, kgrad_two), 'slab')  197 us
    psum x1, waiting for transfers between devices, per_device(): total_one, total_two = lax.psum((factor * sum_one, factor * sum_two), 'pat')  66.8 us
    ppermute x3, starting transfers between devices, padded_2(): before = lax.ppermute(last, axis, up)  13.8 us
  transfers between devices with their start and end apart: 8, of which 3 were waited for; matrix products, arithmetic and copies ran while one was open for 2% of the time, Pallas kernels for 0%

commit v1 on v0

v1 whole, which is shorter than its diff:
```python
import jax
import jax.numpy as jnp
from jax import lax
from jax.experimental import pallas as pl
from jax.experimental.pallas import tpu as pltpu
from jax.sharding import PartitionSpec as P

MESH = pl.DeviceIdType.MESH
C = 64
W = 24
CELLS = 384
PLANES = 6
WIDE = PLANES + 2
TAPS = 9
ROWS = TAPS * C
PADDED = 640
SLABS = 32
PATS = 8
OWNERS = 30
LANE_TILES = 5
BLOCK = (32, 128)
EPS = 1e-05
CLIP = 400.0
RATE = 0.1
COUNT = SLABS * PLANES * CELLS
F32 = jnp.float32
BF16 = jnp.bfloat16


def sigmoid(v):
    return 1.0 / (1.0 + jnp.exp(-v))


def plane(j):
    if isinstance(j, int):
        return pl.ds(j * CELLS, CELLS)
    return pl.ds(pl.multiple_of(j * CELLS, 128), CELLS)


def kernel(
    feat_ref, cot_ref, w_ref, out_ref,
    spread32, feat, cot, masks, kst, kback, im_feat, im_hid, im_cot, parts, normed_one, normed_two, grad,
    lhs, acc, feat_halo, cot_halo, first_halo, second_halo, edge, rows_out, slots, kg, reduced, scaled, pat_slots, gathered,
    halo_send, halo_recv, row_send, row_recv, red_send, red_recv, pat_send, pat_recv, ag_send, ag_recv, core_send, core_recv,
):
    p = lax.axis_index("pat")
    s = lax.axis_index("slab")
    core = lax.rem(p, 2)

    def slab_peer(k):
        return (p, lax.rem(s + k, SLABS))

    def pat_peer(k):
        return (lax.rem(p + k, PATS), s)

    barrier = pltpu.get_barrier_semaphore()

    @pl.loop(1, SLABS)
    def _(k):
        pl.semaphore_signal(barrier, inc=1, device_id=slab_peer(k), device_id_type=MESH)

    @pl.loop(1, PATS)
    def _(k):
        pl.semaphore_signal(barrier, inc=1, device_id=pat_peer(k), device_id_type=MESH)

    def halo_copies(stage, low, high, landing):
        return (
            pltpu.make_async_remote_copy(
                low, landing.at[1], halo_send.at[stage, 0], halo_recv.at[stage, 1],
                device_id=slab_peer(SLABS - 1), device_id_type=MESH,
            ),
            pltpu.make_async_remote_copy(
                high, landing.at[0], halo_send.at[stage, 1], halo_recv.at[stage, 0],
                device_id=slab_peer(1), device_id_type=MESH,
            ),
        )

    def kept(j):
        cut = ((j == 0) & (s == 0)) | ((j == WIDE - 1) & (s == SLABS - 1))
        return jnp.where(cut, 0.0, 1.0).astype(F32)

    def eye():
        i = lax.broadcasted_iota(jnp.int32, (128, 128), 0)
        j = lax.broadcasted_iota(jnp.int32, (128, 128), 1)
        return i == j

    def share_row(r, row):
        rows_out[r] = row

        @pl.loop(1, SLABS)
        def _(k):
            pltpu.make_async_remote_copy(
                rows_out.at[r], slots.at[r, s], row_send.at[r], row_recv.at[r],
                device_id=slab_peer(k), device_id_type=MESH,
            ).start()

        slots[r, s] = row

    def row_total(r):
        most = slots.at[r, pl.ds(0, SLABS - 1)]
        pltpu.make_async_copy(most, most, row_recv.at[r]).wait()
        return jnp.sum(slots[r], axis=0)

    def share_pair(r, one, two):
        column = jnp.concatenate([one, two], axis=0)
        share_row(r, jnp.sum(jnp.where(eye(), column, 0.0), axis=0, keepdims=True))

    def pair_total(r):
        row = row_total(r) * (1.0 / COUNT)
        column = jnp.sum(jnp.where(eye(), row, 0.0), axis=1, keepdims=True)
        return column[:C], column[C:]

    def taps(values, im, j):
        for t in range(TAPS):
            shift = (t // 3 - 1) * W + (t % 3 - 1)
            if shift == 0:
                piece = values
            else:
                piece = pltpu.roll(values, (-shift) % CELLS, 1)
                piece = (piece.reshape(C // 16, 16, CELLS) * masks[t]).reshape(C, CELLS)
            im[t * C : (t + 1) * C, plane(j)] = piece

    def multiply(matrix, im, start, width):
        columns = pl.ds(start if isinstance(start, int) else pl.multiple_of(start, 128), width)
        parts[:, columns] = jnp.dot(matrix, im[0:ROWS, columns], preferred_element_type=F32)

    def combined(j):
        return (
            parts[0:C, plane(j)]
            + parts[C : 2 * C, plane(j + 1)]
            + parts[2 * C : 3 * C, plane(j + 2)]
        )

    def lane_sum(v):
        return v[:, 0:128] + v[:, 128:256] + v[:, 256:384]

    spread32[...] = feat_ref[0].astype(F32)
    for z in range(PLANES):
        feat[:, plane(z + 1)] = spread32[:, z, :].astype(BF16)
    spread32[...] = cot_ref[0].astype(F32)
    for z in range(PLANES):
        cot[:, plane(z + 1)] = spread32[:, z, :].astype(BF16)
    for side, j in ((0, 1), (1, PLANES)):
        edge[side] = feat[:, plane(j)]
        edge[2 + side] = cot[:, plane(j)]

    cell = lax.broadcasted_iota(jnp.int32, (16, CELLS), 1)
    row, col = lax.div(cell, W), lax.rem(cell, W)
    for t in range(TAPS):
        b, e = t // 3 - 1, t % 3 - 1
        inside = (row + b >= 0) & (row + b < CELLS // W) & (col + e >= 0) & (col + e < W)
        masks[t] = jnp.where(inside, 1.0, 0.0).astype(BF16)
    for a in range(3):
        for k in range(2):
            kst[k, a * C : (a + 1) * C, :] = w_ref[k, :, a * ROWS : (a + 1) * ROWS].astype(BF16)
    for im in (im_feat, im_hid):
        im[ROWS:PADDED, :] = jnp.zeros((PADDED - ROWS, WIDE * CELLS), BF16)

    @pl.loop(1, WIDE - 1)
    def _(j):
        taps(feat[:, plane(j)], im_feat, j)

    @pl.loop(0, 3)
    def _(c):
        multiply(kst[0], im_feat, CELLS + c * 2 * CELLS, 2 * CELLS)

    turned = jnp.transpose(w_ref[1].astype(BF16).astype(F32))
    for a in range(3):
        for t in range(TAPS):
            block = turned[(a * TAPS + t) * C : (a * TAPS + t + 1) * C, :]
            u = TAPS - 1 - t
            kback[(2 - a) * C : (3 - a) * C, u * C : (u + 1) * C] = block.astype(BF16)
    for a in range(3):
        for j in range(WIDE):
            if not a <= j < a + PLANES:
                lhs[a * C : (a + 1) * C, plane(j)] = jnp.zeros((C, CELLS), BF16)

    pl.semaphore_wait(barrier, SLABS - 1 + PATS - 1)

    halos = [halo_copies(0, edge.at[0], edge.at[1], feat_halo), halo_copies(1, edge.at[2], edge.at[3], cot_halo)]
    for pair in halos:
        for copy in pair:
            copy.start()
    for copy in halos[0]:
        copy.wait_recv()
    for side, j in ((0, 0), (1, WIDE - 1)):
        taps(feat_halo[side] * kept(j).astype(BF16), im_feat, j)
        multiply(kst[0], im_feat, j * CELLS, CELLS)

    def convolved(target):
        def body(j, carry):
            value = combined(j)
            target[:, plane(j + 1)] = value
            return carry[0] + lane_sum(value), carry[1] + lane_sum(value * value)

        zero = jnp.zeros((C, 128), F32)
        one, two = lax.fori_loop(0, PLANES, body, (zero, zero))
        return jnp.sum(one, axis=1, keepdims=True), jnp.sum(two, axis=1, keepdims=True)

    def exchange(stage, field, landing):
        pair = halo_copies(stage, field.at[:, plane(1)], field.at[:, plane(PLANES)], landing)
        for copy in pair:
            copy.start()
        return pair

    share_pair(0, *convolved(normed_one))
    pair = exchange(2, normed_one, first_halo)
    centre_one, squares = pair_total(0)
    spread_one = lax.rsqrt(squares - centre_one * centre_one + EPS)
    for copy in pair:
        copy.wait()
    normed_one[:, plane(0)] = first_halo[0]
    normed_one[:, plane(WIDE - 1)] = first_halo[1]

    @pl.loop(0, WIDE)
    def _(j):
        value = (normed_one[:, plane(j)] - centre_one) * spread_one
        normed_one[:, plane(j)] = value
        taps((value * sigmoid(value) * kept(j)).astype(BF16), im_hid, j)

    @pl.loop(0, 4)
    def _(c):
        multiply(kst[1], im_hid, c * 2 * CELLS, 2 * CELLS)

    share_pair(1, *convolved(normed_two))
    pair = exchange(3, normed_two, second_halo)
    centre_two, squares = pair_total(1)
    spread_two = lax.rsqrt(squares - centre_two * centre_two + EPS)
    for copy in halos[1]:
        copy.wait()
    for copy in pair:
        copy.wait()
    normed_two[:, plane(0)] = second_halo[0]
    normed_two[:, plane(WIDE - 1)] = second_halo[1]
    cot[:, plane(0)] = cot_halo[0]
    cot[:, plane(WIDE - 1)] = cot_halo[1]

    def slope(v):
        h = sigmoid(v)
        return h * (1.0 + v * (1.0 - h))

    def second_gradient(j, carry):
        value = (normed_two[:, plane(j)] - centre_two) * spread_two
        normed_two[:, plane(j)] = value
        g = cot[:, plane(j)].astype(F32) * slope(value)
        grad[:, plane(j)] = g
        return carry[0] + lane_sum(g), carry[1] + lane_sum(g * value)

    zero = jnp.zeros((C, 128), F32)
    one, two = lax.fori_loop(1, WIDE - 1, second_gradient, (zero, zero))
    share_pair(2, jnp.sum(one, axis=1, keepdims=True), jnp.sum(two, axis=1, keepdims=True))
    second_gradient(0, (zero, zero))
    second_gradient(WIDE - 1, (zero, zero))
    mean_two, cross_two = pair_total(2)

    @pl.loop(0, WIDE)
    def _(j):
        value = spread_two * (grad[:, plane(j)] - mean_two - normed_two[:, plane(j)] * cross_two)
        value = (value * kept(j)).astype(BF16)
        cot[:, plane(j)] = value
        taps(value, im_cot, j)

    @pl.loop(0, 4)
    def _(c):
        multiply(kback[...], im_cot, c * 2 * CELLS, 2 * CELLS)

    def first_gradient(j, carry):
        value = normed_one[:, plane(j + 1)]
        g = combined(j) * slope(value)
        grad[:, plane(j + 1)] = g
        return carry[0] + lane_sum(g), carry[1] + lane_sum(g * value)

    one, two = lax.fori_loop(0, PLANES, first_gradient, (zero, zero))
    share_pair(3, jnp.sum(one, axis=1, keepdims=True), jnp.sum(two, axis=1, keepdims=True))

    def kernel_gradient(k, im):
        @pl.loop(0, 4)
        def _(c):
            columns = pl.ds(pl.multiple_of(c * 2 * CELLS, 128), 2 * CELLS)
            term = lax.dot_general(
                lhs[:, columns], im[:, columns], (((1,), (1,)), ((), ())), preferred_element_type=F32
            )

            @pl.when(c == 0)
            def _():
                acc[...] = term

            @pl.when(c > 0)
            def _():
                acc[...] += term

        for rg in range(6):
            for lt in range(LANE_TILES):
                kg[k, rg * LANE_TILES + lt] = acc[rg * 32 : (rg + 1) * 32, lt * 128 : (lt + 1) * 128]

        @pl.loop(1, SLABS)
        def _(q):
            owner = lax.rem(s + q, SLABS)

            @pl.when(owner < OWNERS)
            def _():
                pltpu.make_async_remote_copy(
                    kg.at[k, owner], reduced.at[k, s], red_send.at[k], red_recv.at[k],
                    device_id=(p, owner), device_id_type=MESH,
                ).start()

        @pl.when(s < OWNERS)
        def _():
            reduced[k, s] = kg[k, s]

    def place(j, value):
        for a in range(3):
            lhs[a * C : (a + 1) * C, plane(j + a)] = value

    @pl.loop(0, PLANES)
    def _(j):
        place(j, cot[:, plane(j + 1)])

    kernel_gradient(1, im_hid)
    mean_one, cross_one = pair_total(3)

    @pl.loop(0, PLANES)
    def _(j):
        value = spread_one * (grad[:, plane(j + 1)] - mean_one - normed_one[:, plane(j + 1)] * cross_one)
        place(j, value.astype(BF16))

    kernel_gradient(0, im_feat)

    def wait_blocks(ref, sem):
        pltpu.make_async_copy(ref, ref, sem).wait()

    @pl.when(s < OWNERS)
    def _():
        for k in (1, 0):
            wait_blocks(reduced.at[k, pl.ds(0, SLABS - 1)], red_recv.at[k])
            scaled[k] = lax.fori_loop(0, SLABS, lambda q, total: total + reduced[k, q], jnp.zeros(BLOCK, F32))

    @pl.when(s >= OWNERS)
    def _():
        for k in (0, 1):
            scaled[k] = jnp.zeros(BLOCK, F32)

    squared = jnp.sum(scaled[0] * scaled[0] + scaled[1] * scaled[1], axis=0, keepdims=True)
    share_row(4, squared)
    length = jnp.sqrt(jnp.sum(row_total(4), axis=1, keepdims=True))
    factor = CLIP / jnp.maximum(length, CLIP)
    for k in (0, 1):
        scaled[k] = scaled[k] * factor

    @pl.when(s < OWNERS)
    def _():
        @pl.loop(1, PATS)
        def _(q):
            peer = lax.rem(p + q, PATS)
            pltpu.make_async_remote_copy(
                scaled.at[lax.rem(peer, 2)], pat_slots.at[p], pat_send, pat_recv,
                device_id=(peer, s), device_id_type=MESH,
            ).start()

        pat_slots[p] = scaled[core]
        wait_blocks(pat_slots.at[pl.ds(0, PATS - 1)], pat_recv)
        total = pat_slots[0]
        for q in range(1, PATS):
            total = total + pat_slots[q]
        gathered[core, s] = total

        @pl.loop(1, SLABS)
        def _(q):
            pltpu.make_async_remote_copy(
                gathered.at[core, s], gathered.at[core, s], ag_send, ag_recv,
                device_id=slab_peer(q), device_id_type=MESH,
            ).start()

        wait_blocks(gathered.at[0, pl.ds(0, OWNERS - 1)], ag_recv)

    @pl.when(s >= OWNERS)
    def _():
        wait_blocks(gathered.at[0, pl.ds(0, OWNERS)], ag_recv)

    last = pltpu.make_async_remote_copy(
        gathered.at[core], gathered.at[core], core_send, core_recv,
        device_id=(p + 1 - 2 * core, s), device_id_type=MESH,
    )
    last.start()
    last.wait()

    for k in range(2):
        for a in range(3):
            for h in range(2):
                for lt in range(LANE_TILES):
                    width = 128 if lt < LANE_TILES - 1 else C
                    start = a * ROWS + lt * 128
                    block = gathered[k, (2 * a + h) * LANE_TILES + lt]
                    out_ref[k, h * 32 : (h + 1) * 32, start : start + width] = block[:, :width]

    for copy in halos[0]:
        copy.wait_send()
    for r in range(5):
        wait_blocks(slots.at[r, pl.ds(0, SLABS - 1)], row_send.at[r])

    @pl.when(s < OWNERS)
    def _():
        for k in range(2):
            wait_blocks(kg.at[k, pl.ds(0, OWNERS - 1)], red_send.at[k])
        wait_blocks(pat_slots.at[pl.ds(0, PATS - 1)], pat_send)
        wait_blocks(reduced.at[0, pl.ds(0, SLABS - 1)], ag_send)

    @pl.when(s >= OWNERS)
    def _():
        for k in range(2):
            wait_blocks(kg.at[k, pl.ds(0, OWNERS)], red_send.at[k])


def clipped_gradients(features, cotangent, weights):
    wide = WIDE * CELLS
    vmem, dma = pltpu.VMEM, pltpu.SemaphoreType.DMA
    return pl.pallas_call(
        kernel,
        out_shape=jax.ShapeDtypeStruct((2, C, 3 * ROWS), F32),
        in_specs=[pl.BlockSpec(memory_space=vmem)] * 3,
        out_specs=pl.BlockSpec(memory_space=vmem),
        scratch_shapes=[
            vmem((C, PLANES, CELLS), F32),
            vmem((C, wide), BF16),
            vmem((C, wide), BF16),
            vmem((TAPS, 16, CELLS), BF16),
            vmem((2, 3 * C, ROWS), BF16),
            vmem((3 * C, ROWS), BF16),
            vmem((PADDED, wide), BF16),
            vmem((PADDED, wide), BF16),
            vmem((ROWS, wide), BF16),
            vmem((3 * C, wide), F32),
            vmem((C, wide), F32),
            vmem((C, wide), F32),
            vmem((C, wide), F32),
            vmem((3 * C, wide), BF16),
            vmem((3 * C, PADDED), F32),
            vmem((2, C, CELLS), BF16),
            vmem((2, C, CELLS), BF16),
            vmem((2, C, CELLS), F32),
            vmem((2, C, CELLS), F32),
            vmem((4, C, CELLS), BF16),
            vmem((5, 1, 128), F32),
            vmem((5, SLABS, 1, 128), F32),
            vmem((2, OWNERS) + BLOCK, F32),
            vmem((2, SLABS) + BLOCK, F32),
            vmem((2,) + BLOCK, F32),
            vmem((PATS,) + BLOCK, F32),
            vmem((2, OWNERS) + BLOCK, F32),
            dma((4, 2)), dma((4, 2)), dma((5,)), dma((5,)), dma((2,)), dma((2,)), dma, dma, dma, dma, dma, dma,
        ],
        compiler_params=pltpu.CompilerParams(
            collective_id=0, has_side_effects=True, vmem_limit_bytes=48 * 1024 * 1024
        ),
    )(features, cotangent, weights)


def per_device(features, cotangent, weights, prev_state, tree_noise):
    total = clipped_gradients(features, cotangent, weights)
    return prev_state + total, weights - RATE * (total + tree_noise)


def solution(mesh):
    return jax.shard_map(
        per_device,
        mesh=mesh,
        in_specs=(P("pat", None, "slab", None), P("pat", None, "slab", None), P(), P(), P()),
        out_specs=(P(), P()),
        check_vma=False,
    )
```

time: 597 us -> 101 us (0.17)
  waiting for transfers between devices: 265 us -> 0 us
  blocking collectives: 233 us -> 0 us
  Pallas kernels: 0 us -> 96.5 us
  other arithmetic: 28.8 us -> 1.42 us
  matrix products: 18.9 us -> 0 us
  starting transfers between devices: 17.7 us -> 0 us
  between operations: 16.2 us -> 0.69 us
  local copies, waits for them, and re-layouts: 15.9 us -> 2.39 us
    psum x2 -> x0, waiting for transfers between devices: 264 us -> none  [the longest x1 197 us: per_device(): sum_one, sum_two = lax.psum((kgrad_one, kgrad_two), 'slab')]
    psum x4 -> x0, blocking collectives: 233 us -> none  [slab_totals(): return lax.psum((first, second), 'slab')]
    pallas_call x0 -> x1, Pallas kernels: none -> 96.5 us  [clipped_gradients(): pl.pallas_call(kernel, out_shape=jax.ShapeDtypeStruct((2, C, 3 * ROWS), F...]
    dot_general x15 -> x0, matrix products: 18.9 us -> none  [the longest x6 11.1 us: kernel_grad(): jnp.einsum('ozp,izp->oi', upstream, stacked, preferred_element_type=jnp.f...]
    ppermute x6 -> x0, starting transfers between devices: 17.6 us -> none  [the longest x3 13.8 us: padded_2(): before = lax.ppermute(last, axis, up)]
    unnamed x28 -> x0, other arithmetic: 7.35 us -> none
    reduce_sum x3 -> x0, other arithmetic: 6.06 us -> none  [the longest x2 3.63 us: per_device(): squared = jnp.sum(sum_one * sum_one) + jnp.sum(sum_two * sum_two)]
  transfers between devices with their start and end apart: 8 -> 0, of which waited for: 3 -> 0; matrix products, arithmetic and copies ran while one was open for 2% -> 0% of each run, Pallas kernels for 0% -> 0%
where the time goes in v1:
time: 101 us
  Pallas kernels  96.5 us (96%)
  local copies, waits for them, and re-layouts  2.39 us (2%)
  other arithmetic  1.42 us (1%)
    pallas_call x1, Pallas kernels, clipped_gradients(): pl.pallas_call(kernel, out_shape=jax.ShapeDtypeStruct((2, C, 3 * ROWS), F...  96.5 us
    unnamed x8, local copies, waits for them, and re-layouts  2.39 us

profile of v1, /device:TPU:1, one launch (start us, length us, event | category | flops | bytes accessed | tf_op | source)
XLA Modules:
  0.0 101.0 jit_solution(10322677065312767322)
XLA Ops:
  0.6 0.0 copy-start
  0.6 1.2 %copy.7.feat_ref = bf16[1,64,6,384]{3,2,1,0:T(8,128)(2,1)S(1)} copy(bf16[1,64,6,384]{3,1,2,0:T(8,128)(2,1)} %param.5) | data formatting | bytes 589824 | tf_op args[0]
  1.9 1.1 %copy.8.cot_ref = bf16[1,64,6,384]{3,2,1,0:T(8,128)(2,1)S(1)} copy(bf16[1,64,6,384]{3,1,2,0:T(8,128)(2,1)} %param.6) | data formatting | bytes 589824 | tf_op args[1]
  3.0 0.0 copy-done
  3.0 0.0 copy-start.1
  3.0 0.0 copy-start.2
  3.0 96.5 %shard_map.68 = f32[2,64,1728]{2,1,0:T(8,128)S(1)} custom-call(bf16[1,64,6,384]{3,2,1,0:T(8,128)(2,1)S(1)} %copy.7.feat_ref, bf16[1,64,6,384]{3,2,1,0:T(8,128)(2,1)S(1)} %copy.8.cot_ref, f32[2,64,1728]{2,1,0:T(8,128)S(1)} %copy-done), custom_call_target="tpu_custom_call" | custom-call | tf_op jit(solution)/shard_map/pallas_call | solution.py:417
  99.6 0.0 copy-done.1
  99.6 0.0 copy-done.2
  99.6 1.4 %multiply_subtract_fusion = (f32[2,64,1728]{2,1,0:T(8,128)}, f32[2,64,1728]{2,1,0:T(8,128)}) fusion(f32[2,64,1728]{2,1,0:T(8,128)S(1)} %copy-done, f32[2,64,1728]{2,1,0:T(8,128)S(1)} %shard_map.68, f32[2,64,1728]{2,1,0:T(8,128)S(1)} %copy-done.1, f32[2,64,1728]{2,1,0:T(8,128)S(1)} %copy-done.2), kind=kLoop, calls=%fused_computation | loop fusion | flops 884736 | bytes 5308416 | tf_op jit(solution)/shard_map/sub | solution.py:460
Async XLA Ops:
  0.6 2.4 %copy-start = (f32[2,64,1728]{2,1,0:T(8,128)S(1)}, f32[2,64,1728]{2,1,0:T(8,128)}, u32[]{:S(2)}) copy-start(f32[2,64,1728]{2,1,0:T(8,128)} %w_ref.1) | copy-start | bytes 2654212
  3.0 96.5 %copy-start.1 = (f32[2,64,1728]{2,1,0:T(8,128)S(1)}, f32[2,64,1728]{2,1,0:T(8,128)}, u32[]{:S(2)}) copy-start(f32[2,64,1728]{2,1,0:T(8,128)} %param.9) | copy-start | bytes 2654212
  3.0 96.5 %copy-start.2 = (f32[2,64,1728]{2,1,0:T(8,128)S(1)}, f32[2,64,1728]{2,1,0:T(8,128)}, u32[]{:S(2)}) copy-start(f32[2,64,1728]{2,1,0:T(8,128)} %param.8) | copy-start | bytes 2654212

commit v2 on v1

v2 whole, which is shorter than its diff:
```python
import jax
import jax.numpy as jnp
from jax import lax
from jax.experimental import pallas as pl
from jax.experimental.pallas import tpu as pltpu
from jax.sharding import PartitionSpec as P

MESH = pl.DeviceIdType.MESH
C = 64
W = 24
CELLS = 384
PLANES = 6
WIDE = PLANES + 2
TAPS = 9
ROWS = TAPS * C
PADDED = 640
SLABS = 32
PATS = 8
OWNERS = 27
LANE_TILES = 9
BLOCK = (32, 128)
EPS = 1e-05
CLIP = 400.0
RATE = 0.1
COUNT = SLABS * PLANES * CELLS
F32 = jnp.float32
BF16 = jnp.bfloat16


def sigmoid(v):
    return 1.0 / (1.0 + jnp.exp(-v))


def plane(j, count=1):
    return slice(j * CELLS, (j + count) * CELLS)


def kernel(
    feat_hbm, cot_hbm, w_hbm, out_ref,
    feat_ref, cot_ref, w_ref,
    cot, masks, kst, kback, im_feat, im_hid, im_cot, parts, normed_one, normed_two, grad,
    lhs, acc, feat_halo, cot_halo, first_halo, second_halo, rows_out, slots, kg, reduced, scaled, pat_slots, gathered, lengths,
    halo_send, halo_recv, row_send, row_recv, red_send, red_recv, pat_send, pat_recv, len_send, len_recv, ag_send, ag_recv, core_send, core_recv, load_sem,
):
    p = lax.axis_index("pat")
    s = lax.axis_index("slab")
    core = lax.rem(p, 2)

    def slab_peer(k):
        return (p, lax.rem(s + k, SLABS))

    def pat_peer(k):
        return (lax.rem(p + k, PATS), s)

    pending = []
    barrier = pltpu.get_barrier_semaphore()

    @pl.loop(1, SLABS)
    def _(k):
        pl.semaphore_signal(barrier, inc=1, device_id=slab_peer(k), device_id_type=MESH)

    @pl.loop(1, PATS)
    def _(k):
        pl.semaphore_signal(barrier, inc=1, device_id=pat_peer(k), device_id_type=MESH)

    loads = [
        pltpu.make_async_copy(source, target, load_sem.at[i])
        for i, (source, target) in enumerate(((feat_hbm, feat_ref), (w_hbm, w_ref), (cot_hbm, cot_ref)))
    ]
    for load in loads:
        load.start()

    def halo_copies(stage, low, high, landing):
        return (
            pltpu.make_async_remote_copy(
                low, landing.at[1], halo_send.at[stage, 0], halo_recv.at[stage, 1],
                device_id=slab_peer(SLABS - 1), device_id_type=MESH,
            ),
            pltpu.make_async_remote_copy(
                high, landing.at[0], halo_send.at[stage, 1], halo_recv.at[stage, 0],
                device_id=slab_peer(1), device_id_type=MESH,
            ),
        )

    def wait_blocks(ref, sem):
        pltpu.make_async_copy(ref, ref, sem).wait()

    def wait_owned(ref, sem):
        @pl.when(s < OWNERS)
        def _():
            wait_blocks(ref.at[pl.ds(0, OWNERS - 1)], sem)

        @pl.when(s >= OWNERS)
        def _():
            wait_blocks(ref.at[pl.ds(0, OWNERS)], sem)

    def wait_red(k):
        @pl.when(s < OWNERS)
        def _():
            wait_blocks(reduced.at[k, pl.ds(0, SLABS - 1)], red_recv.at[k])

    def kept(j):
        if 0 < j < WIDE - 1:
            return 1.0
        return jnp.where(s == (0 if j == 0 else SLABS - 1), 0.0, 1.0).astype(F32)

    def eye():
        i = lax.broadcasted_iota(jnp.int32, (128, 128), 0)
        j = lax.broadcasted_iota(jnp.int32, (128, 128), 1)
        return i == j

    def share_row(r, row):
        rows_out[r] = row

        @pl.loop(1, SLABS)
        def _(k):
            pltpu.make_async_remote_copy(
                rows_out.at[r], slots.at[r, s], row_send.at[r], row_recv.at[r],
                device_id=slab_peer(k), device_id_type=MESH,
            ).start()

        slots[r, s] = row
        pending.append(lambda: wait_blocks(slots.at[r, pl.ds(0, SLABS - 1)], row_send.at[r]))

    def row_total(r):
        most = slots.at[r, pl.ds(0, SLABS - 1)]
        pltpu.make_async_copy(most, most, row_recv.at[r]).wait()
        return jnp.sum(slots[r], axis=0)

    def share_pair(r, one, two):
        column = jnp.concatenate([one, two], axis=0)
        share_row(r, jnp.sum(jnp.where(eye(), column, 0.0), axis=0, keepdims=True))

    def pair_total(r):
        row = row_total(r) * (1.0 / COUNT)
        column = jnp.sum(jnp.where(eye(), row, 0.0), axis=1, keepdims=True)
        return column[:C], column[C:]

    def taps(values, im, j):
        for t in range(TAPS):
            shift = (t // 3 - 1) * W + (t % 3 - 1)
            if shift == 0:
                piece = values
            else:
                piece = pltpu.roll(values, (-shift) % CELLS, 1)
                piece = (piece.reshape(C // 16, 16, CELLS) * masks[t]).reshape(C, CELLS)
            im[t * C : (t + 1) * C, plane(j)] = piece

    def multiply(matrix, im, first, count):
        parts[:, plane(first, count)] = jnp.dot(matrix, im[0:ROWS, plane(first, count)], preferred_element_type=F32)

    def combined(j):
        return (
            parts[0:C, plane(j)]
            + parts[C : 2 * C, plane(j + 1)]
            + parts[2 * C : 3 * C, plane(j + 2)]
        )

    def lane_sum(v):
        return v[:, 0:128] + v[:, 128:256] + v[:, 256:384]

    cell = lax.broadcasted_iota(jnp.int32, (16, CELLS), 1)
    row, col = lax.div(cell, W), lax.rem(cell, W)
    for t in range(TAPS):
        b, e = t // 3 - 1, t % 3 - 1
        inside = (row + b >= 0) & (row + b < CELLS // W) & (col + e >= 0) & (col + e < W)
        masks[t] = jnp.where(inside, 1.0, 0.0).astype(BF16)
    loads[1].wait()
    for a in range(3):
        kst[0, a * C : (a + 1) * C, :] = w_ref[0, :, a * ROWS : (a + 1) * ROWS].astype(BF16)
    loads[0].wait()
    for j in range(1, WIDE - 1):
        taps(feat_ref[j - 1], im_feat, j)
    loads[2].wait()
    pl.semaphore_wait(barrier, SLABS - 1 + PATS - 1)

    halos = [halo_copies(0, feat_ref.at[0], feat_ref.at[PLANES - 1], feat_halo), halo_copies(1, cot_ref.at[0], cot_ref.at[PLANES - 1], cot_halo)]
    for pair in halos:
        for copy in pair:
            copy.start()
    multiply(kst[0], im_feat, 1, PLANES)
    for copy in halos[0]:
        copy.wait_recv()
        pending.append(copy.wait_send)
    for side, j, a in ((0, 0, 0), (1, WIDE - 1, 2)):
        taps(feat_halo[side] * kept(j).astype(BF16), im_feat, j)
        parts[a * C : (a + 1) * C, plane(j)] = jnp.dot(
            kst[0, a * C : (a + 1) * C, :], im_feat[0:ROWS, plane(j)], preferred_element_type=F32
        )

    def convolved(target, stage, landing):
        one = two = jnp.zeros((C, 128), F32)
        for z in (0, PLANES - 1, 1, 2, 3, 4):
            value = combined(z)
            target[:, plane(z + 1)] = value
            one, two = one + lane_sum(value), two + lane_sum(value * value)
            if z == PLANES - 1:
                pair = halo_copies(stage, target.at[:, plane(1)], target.at[:, plane(PLANES)], landing)
                for copy in pair:
                    copy.start()
        return pair, jnp.sum(one, axis=1, keepdims=True), jnp.sum(two, axis=1, keepdims=True)

    pair, *sums = convolved(normed_one, 2, first_halo)
    share_pair(0, *sums)

    for a in range(3):
        kst[1, a * C : (a + 1) * C, :] = w_ref[1, :, a * ROWS : (a + 1) * ROWS].astype(BF16)
    turned = jnp.transpose(w_ref[1].astype(BF16).astype(F32))
    for a in range(3):
        for t in range(TAPS):
            block = turned[(a * TAPS + t) * C : (a * TAPS + t + 1) * C, :]
            u = TAPS - 1 - t
            kback[(2 - a) * C : (3 - a) * C, u * C : (u + 1) * C] = block.astype(BF16)
        for j in range(WIDE):
            if not a <= j < a + PLANES:
                lhs[a * C : (a + 1) * C, plane(j)] = jnp.zeros((C, CELLS), BF16)
    for im in (im_feat, im_hid):
        im[ROWS:PADDED, :] = jnp.zeros((PADDED - ROWS, WIDE * CELLS), BF16)

    centre_one, squares = pair_total(0)
    spread_one = lax.rsqrt(squares - centre_one * centre_one + EPS)
    for copy in pair:
        copy.wait()
    normed_one[:, plane(0)] = first_halo[0]
    normed_one[:, plane(WIDE - 1)] = first_halo[1]

    for j in range(WIDE):
        value = (normed_one[:, plane(j)] - centre_one) * spread_one
        normed_one[:, plane(j)] = value
        taps((value * sigmoid(value) * kept(j)).astype(BF16), im_hid, j)
        if j % 2:
            multiply(kst[1], im_hid, j - 1, 2)

    pair, *sums = convolved(normed_two, 3, second_halo)
    share_pair(1, *sums)
    centre_two, squares = pair_total(1)
    spread_two = lax.rsqrt(squares - centre_two * centre_two + EPS)
    for copy in halos[1]:
        copy.wait()
    for copy in pair:
        copy.wait()
    normed_two[:, plane(0)] = second_halo[0]
    normed_two[:, plane(WIDE - 1)] = second_halo[1]

    def slope(v):
        h = sigmoid(v)
        return h * (1.0 + v * (1.0 - h))

    def second_gradient(j, carry, upstream=None):
        value = (normed_two[:, plane(j)] - centre_two) * spread_two
        normed_two[:, plane(j)] = value
        upstream = cot_ref[j - 1] if upstream is None else upstream
        g = upstream.astype(F32) * slope(value)
        grad[:, plane(j)] = g
        return carry[0] + lane_sum(g), carry[1] + lane_sum(g * value)

    zero = jnp.zeros((C, 128), F32)
    carry = (zero, zero)
    for j in range(1, WIDE - 1):
        carry = second_gradient(j, carry)
    one, two = carry
    share_pair(2, jnp.sum(one, axis=1, keepdims=True), jnp.sum(two, axis=1, keepdims=True))
    second_gradient(0, (zero, zero), cot_halo[0])
    second_gradient(WIDE - 1, (zero, zero), cot_halo[1])
    mean_two, cross_two = pair_total(2)

    for j in range(WIDE):
        value = spread_two * (grad[:, plane(j)] - mean_two - normed_two[:, plane(j)] * cross_two)
        value = (value * kept(j)).astype(BF16)
        cot[:, plane(j)] = value
        taps(value, im_cot, j)
        if j % 2:
            multiply(kback[...], im_cot, j - 1, 2)

    def first_gradient(j, carry):
        value = normed_one[:, plane(j + 1)]
        g = combined(j) * slope(value)
        grad[:, plane(j + 1)] = g
        return carry[0] + lane_sum(g), carry[1] + lane_sum(g * value)

    carry = (zero, zero)
    for z in range(PLANES):
        carry = first_gradient(z, carry)
    one, two = carry
    share_pair(3, jnp.sum(one, axis=1, keepdims=True), jnp.sum(two, axis=1, keepdims=True))

    def kernel_gradient(k, im):
        def send(first, count):
            for a in range(3):
                for t in range(first, first + count):
                    owner = a * LANE_TILES + t

                    @pl.when(s != owner)
                    def _():
                        pltpu.make_async_remote_copy(
                            kg.at[k, owner], reduced.at[k, s], red_send.at[k], red_recv.at[k],
                            device_id=(p, owner), device_id_type=MESH,
                        ).start()

        for first in (0, 256, 512):
            width = 256 if first < 512 else 128
            term = lax.dot_general(
                lhs[...], im[first : first + width, :], (((1,), (1,)), ((), ())), preferred_element_type=F32
            )
            for a in range(3):
                low, high = term[a * C : a * C + 32], term[a * C + 32 : (a + 1) * C]
                if first < 512:
                    for t in range(2):
                        lanes = slice(t * 128, (t + 1) * 128)
                        kg[k, a * LANE_TILES + first // 128 + t] = low[:, lanes].astype(BF16)
                        kg[k, a * LANE_TILES + 4 + first // 128 + t] = high[:, lanes].astype(BF16)
                else:
                    kg[k, a * LANE_TILES + 8] = (low + pltpu.roll(high, C, 1)).astype(BF16)
            if first < 512:
                send(first // 128, 2)
                send(4 + first // 128, 2)
            else:
                send(8, 1)

        @pl.when(s < OWNERS)
        def _():
            reduced[k, s] = kg[k, s]

        pending.append(lambda: wait_owned(kg.at[k], red_send.at[k]))

    def place(j, value):
        for a in range(3):
            lhs[a * C : (a + 1) * C, plane(j + a)] = value

    for j in range(PLANES):
        place(j, cot[:, plane(j + 1)])

    kernel_gradient(1, im_hid)
    mean_one, cross_one = pair_total(3)

    for j in range(PLANES):
        value = spread_one * (grad[:, plane(j + 1)] - mean_one - normed_one[:, plane(j + 1)] * cross_one)
        place(j, value.astype(BF16))

    kernel_gradient(0, im_feat)

    @pl.when(s < OWNERS)
    def _():
        for k in (1, 0):
            wait_red(k)
            scaled[k] = lax.fori_loop(0, SLABS, lambda q, total: total + reduced[k, q].astype(F32), jnp.zeros(BLOCK, F32))

    @pl.when(s >= OWNERS)
    def _():
        for k in (0, 1):
            scaled[k] = jnp.zeros(BLOCK, F32)

    squared = jnp.sum(scaled[0] * scaled[0] + scaled[1] * scaled[1], axis=0, keepdims=True)
    share_row(4, squared)

    @pl.when(s < OWNERS)
    def _():
        @pl.loop(1, PATS)
        def _(q):
            peer = lax.rem(p + q, PATS)
            pltpu.make_async_remote_copy(
                scaled.at[lax.rem(peer, 2)], pat_slots.at[p], pat_send, pat_recv,
                device_id=(peer, s), device_id_type=MESH,
            ).start()

        pat_slots[p] = scaled[core]

    lengths[p] = row_total(4)

    @pl.when(s < OWNERS)
    def _():
        @pl.loop(1, PATS)
        def _(q):
            pltpu.make_async_remote_copy(
                lengths.at[p], lengths.at[p], len_send, len_recv, device_id=pat_peer(q), device_id_type=MESH
            ).start()

        wait_blocks(pat_slots.at[pl.ds(0, PATS - 1)], pat_recv)
        wait_blocks(lengths.at[pl.ds(0, PATS - 1)], len_recv)
        wait_blocks(lengths.at[pl.ds(0, PATS - 1)], len_send)
        total = jnp.zeros(BLOCK, F32)
        for q in range(PATS):
            length = jnp.sqrt(jnp.sum(lengths[q], axis=1, keepdims=True))
            total = total + (CLIP / jnp.maximum(length, CLIP)) * pat_slots[q]
        gathered[core, s] = total.astype(BF16)
        wait_blocks(pat_slots.at[pl.ds(0, PATS - 1)], pat_send)


    @pl.when(s < OWNERS)
    def _():
        @pl.loop(1, SLABS)
        def _(q):
            pltpu.make_async_remote_copy(
                gathered.at[core, s], gathered.at[core, s], ag_send, ag_recv,
                device_id=slab_peer(q), device_id_type=MESH,
            ).start()

    wait_owned(gathered.at[0], ag_recv)

    last = pltpu.make_async_remote_copy(
        gathered.at[core], gathered.at[core], core_send, core_recv,
        device_id=(p + 1 - 2 * core, s), device_id_type=MESH,
    )
    last.start()
    last.wait()

    for k in range(2):
        for a in range(3):
            for t in range(LANE_TILES):
                block = gathered[k, a * LANE_TILES + t].astype(F32)
                start = a * ROWS + t % 4 * 128
                if t < 4:
                    out_ref[k, 0:32, start : start + 128] = block
                elif t < 8:
                    out_ref[k, 32:C, start : start + 128] = block
                else:
                    out_ref[k, 0:32, start + 512 : start + ROWS] = block[:, :C]
                    out_ref[k, 32:C, start + 512 : start + ROWS] = block[:, C:]

    @pl.when(s < OWNERS)
    def _():
        wait_blocks(reduced.at[0, pl.ds(0, SLABS - 1)], ag_send)

    for wait in pending:
        wait()


def clipped_gradients(features, cotangent, weights):
    wide = WIDE * CELLS
    vmem, dma = pltpu.VMEM, pltpu.SemaphoreType.DMA
    return pl.pallas_call(
        kernel,
        out_shape=jax.ShapeDtypeStruct((2, C, 3 * ROWS), F32),
        in_specs=[pl.BlockSpec(memory_space=pltpu.HBM)] * 3,
        out_specs=pl.BlockSpec(memory_space=vmem),
        scratch_shapes=[
            vmem((PLANES, C, CELLS), BF16),
            vmem((PLANES, C, CELLS), BF16),
            vmem((2, C, 3 * ROWS), F32),
            vmem((C, wide), BF16),
            vmem((TAPS, 16, CELLS), BF16),
            vmem((2, 3 * C, ROWS), BF16),
            vmem((3 * C, ROWS), BF16),
            vmem((PADDED, wide), BF16),
            vmem((PADDED, wide), BF16),
            vmem((ROWS, wide), BF16),
            vmem((3 * C, wide), F32),
            vmem((C, wide), F32),
            vmem((C, wide), F32),
            vmem((C, wide), F32),
            vmem((3 * C, wide), BF16),
            vmem((3 * C, PADDED), F32),
            vmem((2, C, CELLS), BF16),
            vmem((2, C, CELLS), BF16),
            vmem((2, C, CELLS), F32),
            vmem((2, C, CELLS), F32),
            vmem((5, 1, 128), F32),
            vmem((5, SLABS, 1, 128), F32),
            vmem((2, OWNERS) + BLOCK, BF16),
            vmem((2, SLABS) + BLOCK, BF16),
            vmem((2,) + BLOCK, F32),
            vmem((PATS,) + BLOCK, F32),
            vmem((2, OWNERS) + BLOCK, BF16),
            vmem((PATS, 1, 128), F32),
            dma((4, 2)), dma((4, 2)), dma((5,)), dma((5,)), dma((2,)), dma((2,)), dma, dma, dma, dma, dma, dma, dma, dma, dma((3,)),
        ],
        compiler_params=pltpu.CompilerParams(
            collective_id=0, has_side_effects=True, vmem_limit_bytes=32 * 1024 * 1024
        ),
    )(features, cotangent, weights)


def per_device(features, cotangent, weights, prev_state, tree_noise):
    planes = (features[0].transpose(1, 0, 2), cotangent[0].transpose(1, 0, 2), weights)
    total = clipped_gradients(*(pltpu.with_memory_space_constraint(v, pltpu.HBM) for v in planes))
    return prev_state + total, weights - RATE * (total + tree_noise)


def solution(mesh):
    return jax.shard_map(
        per_device,
        mesh=mesh,
        in_specs=(P("pat", None, "slab", None), P("pat", None, "slab", None), P(), P(), P()),
        out_specs=(P(), P()),
        check_vma=False,
    )
```

time: 101 us -> 79 us (0.78)
  Pallas kernels: 96.5 us -> 75.6 us
  local copies, waits for them, and re-layouts: 2.39 us -> 0.01 us
  other arithmetic: 1.42 us -> 2.6 us
    pallas_call x1, Pallas kernels: 96.5 us -> 75.6 us  [clipped_gradients(): pl.pallas_call(kernel, out_shape=jax.ShapeDtypeStruct((2, C, 3 * ROWS), F...]
    unnamed x8 -> x4, local copies, waits for them, and re-layouts: 2.39 us -> 0.01 us
    sub x1, other arithmetic: 1.42 us -> 2.6 us  [per_device(): return (prev_state + total, weights - RATE * (total + tree_noise))]
where the time goes in v2:
time: 79 us; the launch traced here: 78.9 us
  Pallas kernels  75.6 us (96%)
  other arithmetic  2.6 us (3%)
    pallas_call x1, Pallas kernels, clipped_gradients(): pl.pallas_call(kernel, out_shape=jax.ShapeDtypeStruct((2, C, 3 * ROWS), F...  75.6 us
    sub x1, other arithmetic, per_device(): return (prev_state + total, weights - RATE * (total + tree_noise))  2.6 us

profile of v2, /device:TPU:1, one launch (start us, length us, event | category | flops | bytes accessed | tf_op | source)
XLA Modules:
  0.0 78.9 jit_solution(3601586400493324305)
XLA Ops:
  0.6 0.0 copy-start
  0.6 0.0 copy-start.1
  0.7 75.6 %shard_map.68 = f32[2,64,1728]{2,1,0:T(8,128)S(1)} custom-call(bf16[6,64,384]{2,1,0:T(8,128)(2,1)} %bitcast.6, bf16[6,64,384]{2,1,0:T(8,128)(2,1)} %bitcast.7, f32[2,64,1728]{2,1,0:T(8,128)} %w_hbm.1), custom_call_target="tpu_custom_call" | custom-call | tf_op jit(solution)/shard_map/pallas_call | solution.py:431
  76.2 0.0 copy-done
  76.3 0.0 copy-done.1
  76.3 2.6 %multiply_subtract_fusion = (f32[2,64,1728]{2,1,0:T(8,128)}, f32[2,64,1728]{2,1,0:T(8,128)}) fusion(f32[2,64,1728]{2,1,0:T(8,128)S(1)} %copy-done, f32[2,64,1728]{2,1,0:T(8,128)S(1)} %shard_map.68, f32[2,64,1728]{2,1,0:T(8,128)S(1)} %copy-done.1, f32[2,64,1728]{2,1,0:T(8,128)} %param.8), kind=kLoop, calls=%fused_computation | loop fusion | flops 884736 | bytes 5308416 | tf_op jit(solution)/shard_map/sub | solution.py:476
Async XLA Ops:
  0.6 75.6 %copy-start = (f32[2,64,1728]{2,1,0:T(8,128)S(1)}, f32[2,64,1728]{2,1,0:T(8,128)}, u32[]{:S(2)}) copy-start(f32[2,64,1728]{2,1,0:T(8,128)} %w_hbm.1) | copy-start | bytes 2654212
  0.6 75.6 %copy-start.1 = (f32[2,64,1728]{2,1,0:T(8,128)S(1)}, f32[2,64,1728]{2,1,0:T(8,128)}, u32[]{:S(2)}) copy-start(f32[2,64,1728]{2,1,0:T(8,128)} %param.9) | copy-start | bytes 2654212

commit v3 on v2

--- a/solution.py
+++ b/solution.py
@@ -14,7 +14,9 @@
 TAPS = 9
 ROWS = TAPS * C
 PADDED = 640
-SLABS = 32
+DEEP = 8
+TALL = 4
+SLABS = TALL * DEEP
 PATS = 8
 OWNERS = 27
 LANE_TILES = 9
@@ -27,6 +29,11 @@
 BF16 = jnp.bfloat16
 
 
+def far_first():
+    steps = [(dy, dz) for dy in range(TALL) for dz in range(DEEP) if dy or dz]
+    return sorted(steps, key=lambda d: -min(d[0], TALL - d[0]) - min(d[1], DEEP - d[1]))
+
+
 def sigmoid(v):
     return 1.0 / (1.0 + jnp.exp(-v))
 
@@ -36,15 +43,21 @@
 
 
 def kernel(
-    feat_hbm, cot_hbm, w_hbm, out_ref,
-    feat_ref, cot_ref, w_ref,
+    feat_hbm, cot_hbm, w_hbm, noise_hbm, out_ref, stepped_ref,
+    feat_ref, cot_ref, w_ref, noise_ref,
     cot, masks, kst, kback, im_feat, im_hid, im_cot, parts, normed_one, normed_two, grad,
     lhs, acc, feat_halo, cot_halo, first_halo, second_halo, rows_out, slots, kg, reduced, scaled, pat_slots, gathered, lengths,
-    halo_send, halo_recv, row_send, row_recv, red_send, red_recv, pat_send, pat_recv, len_send, len_recv, ag_send, ag_recv, core_send, core_recv, load_sem,
+    halo_send, halo_recv, row_send, row_recv, red_send, red_recv, pat_send, pat_recv, len_send, len_recv, deep_send, deep_recv, tall_send, tall_recv, core_send, core_recv, load_sem,
 ):
     p = lax.axis_index("pat")
     s = lax.axis_index("slab")
     core = lax.rem(p, 2)
+    y, z = lax.div(s, DEEP), lax.rem(s, DEEP)
+
+    def peer(dy, dz):
+        return (p, lax.rem(y + dy, TALL) * DEEP + lax.rem(z + dz, DEEP))
+
+    slab_peers = [peer(dy, dz) for dy, dz in far_first()]
 
     def slab_peer(k):
         return (p, lax.rem(s + k, SLABS))
@@ -55,9 +68,8 @@
     pending = []
     barrier = pltpu.get_barrier_semaphore()
 
-    @pl.loop(1, SLABS)
-    def _(k):
-        pl.semaphore_signal(barrier, inc=1, device_id=slab_peer(k), device_id_type=MESH)
+    for other in slab_peers:
+        pl.semaphore_signal(barrier, inc=1, device_id=other, device_id_type=MESH)
 
     @pl.loop(1, PATS)
     def _(k):
@@ -65,9 +77,9 @@
 
     loads = [
         pltpu.make_async_copy(source, target, load_sem.at[i])
-        for i, (source, target) in enumerate(((feat_hbm, feat_ref), (w_hbm, w_ref), (cot_hbm, cot_ref)))
+        for i, (source, target) in enumerate(((feat_hbm, feat_ref), (w_hbm, w_ref), (cot_hbm, cot_ref), (noise_hbm, noise_ref)))
     ]
-    for load in loads:
+    for load in loads[:2]:
         load.start()
 
     def halo_copies(stage, low, high, landing):
@@ -112,11 +124,10 @@
     def share_row(r, row):
         rows_out[r] = row
 
-        @pl.loop(1, SLABS)
-        def _(k):
+        for other in slab_peers:
             pltpu.make_async_remote_copy(
                 rows_out.at[r], slots.at[r, s], row_send.at[r], row_recv.at[r],
-                device_id=slab_peer(k), device_id_type=MESH,
+                device_id=other, device_id_type=MESH,
             ).start()
 
         slots[r, s] = row
@@ -169,15 +180,15 @@
     for a in range(3):
         kst[0, a * C : (a + 1) * C, :] = w_ref[0, :, a * ROWS : (a + 1) * ROWS].astype(BF16)
     loads[0].wait()
+    for load in loads[2:]:
+        load.start()
     for j in range(1, WIDE - 1):
         taps(feat_ref[j - 1], im_feat, j)
-    loads[2].wait()
     pl.semaphore_wait(barrier, SLABS - 1 + PATS - 1)
 
     halos = [halo_copies(0, feat_ref.at[0], feat_ref.at[PLANES - 1], feat_halo), halo_copies(1, cot_ref.at[0], cot_ref.at[PLANES - 1], cot_halo)]
-    for pair in halos:
-        for copy in pair:
-            copy.start()
+    for copy in halos[0]:
+        copy.start()
     multiply(kst[0], im_feat, 1, PLANES)
     for copy in halos[0]:
         copy.wait_recv()
@@ -203,6 +214,12 @@
     pair, *sums = convolved(normed_one, 2, first_halo)
     share_pair(0, *sums)
 
+    for k in range(2):
+        for slot in range(OWNERS, SLABS):
+            gathered[k, slot] = jnp.zeros(BLOCK, BF16)
+    for load in loads[2:]:
+        load.wait()
+    stepped_ref[...] = w_ref[...] - RATE * noise_ref[...]
     for a in range(3):
         kst[1, a * C : (a + 1) * C, :] = w_ref[1, :, a * ROWS : (a + 1) * ROWS].astype(BF16)
     turned = jnp.transpose(w_ref[1].astype(BF16).astype(F32))
@@ -218,6 +235,8 @@
         im[ROWS:PADDED, :] = jnp.zeros((PADDED - ROWS, WIDE * CELLS), BF16)
 
     centre_one, squares = pair_total(0)
+    for copy in halos[1]:
+        copy.start()
     spread_one = lax.rsqrt(squares - centre_one * centre_one + EPS)
     for copy in pair:
         copy.wait()
@@ -279,8 +298,8 @@
         return carry[0] + lane_sum(g), carry[1] + lane_sum(g * value)
 
     carry = (zero, zero)
-    for z in range(PLANES):
-        carry = first_gradient(z, carry)
+    for j in range(PLANES):
+        carry = first_gradient(j, carry)
     one, two = carry
     share_pair(3, jnp.sum(one, axis=1, keepdims=True), jnp.sum(two, axis=1, keepdims=True))
 
@@ -343,7 +362,7 @@
     def _():
         for k in (1, 0):
             wait_red(k)
-            scaled[k] = lax.fori_loop(0, SLABS, lambda q, total: total + reduced[k, q].astype(F32), jnp.zeros(BLOCK, F32))
+            scaled[k] = jnp.sum(reduced[k].astype(F32), axis=0)
 
     @pl.when(s >= OWNERS)
     def _():
@@ -386,25 +405,55 @@
         wait_blocks(pat_slots.at[pl.ds(0, PATS - 1)], pat_send)
 
 
+    def forward(slot):
+        for dy in (2, 1, 3):
+            pltpu.make_async_remote_copy(
+                gathered.at[core, slot], gathered.at[core, slot], tall_send.at[dy], tall_recv.at[dy],
+                device_id=peer(dy, 0), device_id_type=MESH,
+            ).start()
+
     @pl.when(s < OWNERS)
     def _():
-        @pl.loop(1, SLABS)
-        def _(q):
-            pltpu.make_async_remote_copy(
-                gathered.at[core, s], gathered.at[core, s], ag_send, ag_recv,
-                device_id=slab_peer(q), device_id_type=MESH,
+        for dz in (4, 3, 5, 2, 6, 1, 7):
+            pltpu.make_async_remote_copy(
+                gathered.at[core, s], gathered.at[core, s], deep_send.at[dz], deep_recv.at[dz],
+                device_id=peer(0, dz), device_id_type=MESH,
             ).start()
-
-    wait_owned(gathered.at[0], ag_recv)
-
-    last = pltpu.make_async_remote_copy(
-        gathered.at[core], gathered.at[core], core_send, core_recv,
-        device_id=(p + 1 - 2 * core, s), device_id_type=MESH,
-    )
-    last.start()
-    last.wait()
-
-    for k in range(2):
+        forward(s)
+
+    for dz in (1, 7, 2, 6, 3, 5, 4):
+        slot = y * DEEP + lax.rem(z + DEEP - dz, DEEP)
+
+        @pl.when(slot < OWNERS)
+        def _():
+            wait_blocks(gathered.at[core, slot], deep_recv.at[dz])
+            forward(slot)
+
+    def wait_row(owner, sem):
+        @pl.when(owner < TALL - 1)
+        def _():
+            wait_blocks(gathered.at[0, 0:DEEP], sem)
+
+        @pl.when(owner == TALL - 1)
+        def _():
+            wait_blocks(gathered.at[0, 0 : OWNERS - DEEP * (TALL - 1)], sem)
+
+    def hand_over(dy):
+        row = lax.rem(y + TALL - dy, TALL)
+        blocks = gathered.at[core, pl.ds(row * DEEP, DEEP)]
+        copy = pltpu.make_async_remote_copy(
+            blocks, blocks, core_send.at[dy], core_recv.at[dy],
+            device_id=(p + 1 - 2 * core, s), device_id_type=MESH,
+        )
+        copy.start()
+        return copy
+
+    rows = [hand_over(0)]
+    for dy in (1, 3, 2):
+        wait_row(lax.rem(y + TALL - dy, TALL), tall_recv.at[dy])
+        rows.append(hand_over(dy))
+
+    def assemble(k):
         for a in range(3):
             for t in range(LANE_TILES):
                 block = gathered[k, a * LANE_TILES + t].astype(F32)
@@ -417,25 +466,34 @@
                     out_ref[k, 0:32, start + 512 : start + ROWS] = block[:, :C]
                     out_ref[k, 32:C, start + 512 : start + ROWS] = block[:, C:]
 
+    assemble(core)
+    for copy in rows:
+        copy.wait()
+    assemble(1 - core)
+
     @pl.when(s < OWNERS)
     def _():
-        wait_blocks(reduced.at[0, pl.ds(0, SLABS - 1)], ag_send)
-
+        for dz in range(1, DEEP):
+            wait_blocks(gathered.at[0, 0], deep_send.at[dz])
+
+    for dy in range(1, TALL):
+        wait_row(y, tall_send.at[dy])
     for wait in pending:
         wait()
 
 
-def clipped_gradients(features, cotangent, weights):
+def clipped_gradients(features, cotangent, weights, tree_noise):
     wide = WIDE * CELLS
     vmem, dma = pltpu.VMEM, pltpu.SemaphoreType.DMA
     return pl.pallas_call(
         kernel,
-        out_shape=jax.ShapeDtypeStruct((2, C, 3 * ROWS), F32),
-        in_specs=[pl.BlockSpec(memory_space=pltpu.HBM)] * 3,
-        out_specs=pl.BlockSpec(memory_space=vmem),
+        out_shape=[jax.ShapeDtypeStruct((2, C, 3 * ROWS), F32)] * 2,
+        in_specs=[pl.BlockSpec(memory_space=pltpu.HBM)] * 4,
+        out_specs=[pl.BlockSpec(memory_space=vmem)] * 2,
         scratch_shapes=[
             vmem((PLANES, C, CELLS), BF16),
             vmem((PLANES, C, CELLS), BF16),
+            vmem((2, C, 3 * ROWS), F32),
             vmem((2, C, 3 * ROWS), F32),
             vmem((C, wide), BF16),
             vmem((TAPS, 16, CELLS), BF16),
@@ -460,20 +518,20 @@
             vmem((2, SLABS) + BLOCK, BF16),
             vmem((2,) + BLOCK, F32),
             vmem((PATS,) + BLOCK, F32),
-            vmem((2, OWNERS) + BLOCK, BF16),
+            vmem((2, SLABS) + BLOCK, BF16),
             vmem((PATS, 1, 128), F32),
-            dma((4, 2)), dma((4, 2)), dma((5,)), dma((5,)), dma((2,)), dma((2,)), dma, dma, dma, dma, dma, dma, dma, dma, dma((3,)),
+            dma((4, 2)), dma((4, 2)), dma((5,)), dma((5,)), dma((2,)), dma((2,)), dma, dma, dma, dma, dma((DEEP,)), dma((DEEP,)), dma((TALL,)), dma((TALL,)), dma((TALL,)), dma((TALL,)), dma((4,)),
         ],
         compiler_params=pltpu.CompilerParams(
             collective_id=0, has_side_effects=True, vmem_limit_bytes=32 * 1024 * 1024
         ),
-    )(features, cotangent, weights)
+    )(features, cotangent, weights, tree_noise)
 
 
 def per_device(features, cotangent, weights, prev_state, tree_noise):
-    planes = (features[0].transpose(1, 0, 2), cotangent[0].transpose(1, 0, 2), weights)
-    total = clipped_gradients(*(pltpu.with_memory_space_constraint(v, pltpu.HBM) for v in planes))
-    return prev_state + total, weights - RATE * (total + tree_noise)
+    planes = (features[0].transpose(1, 0, 2), cotangent[0].transpose(1, 0, 2), weights, tree_noise)
+    total, stepped = clipped_gradients(*(pltpu.with_memory_space_constraint(v, pltpu.HBM) for v in planes))
+    return prev_state + total, stepped - RATE * total
 
 
 def solution(mesh):

time: 79 us -> 76.5 us (0.968)
  other arithmetic: 2.6 us -> 1.4 us
  Pallas kernels: 75.6 us -> 74.4 us
    pallas_call x1, Pallas kernels: 75.6 us -> 74.4 us  [clipped_gradients(): pl.pallas_call(kernel, out_shape=[jax.ShapeDtypeStruct((2, C, 3 * ROWS),...]
    sub x1, other arithmetic: 2.6 us -> 1.4 us  [per_device(): return (prev_state + total, stepped - RATE * total)]
where the time goes in v3:
time: 76.5 us; the launch traced here: 76.4 us
  Pallas kernels  74.4 us (97%)
  other arithmetic  1.4 us (2%)
    pallas_call x1, Pallas kernels, clipped_gradients(): pl.pallas_call(kernel, out_shape=[jax.ShapeDtypeStruct((2, C, 3 * ROWS),...  74.4 us

profile of v3, /device:TPU:1, one launch (start us, length us, event | category | flops | bytes accessed | tf_op | source)
XLA Modules:
  0.0 76.4 jit_solution(938562226913838734)
XLA Ops:
  0.6 0.0 copy-start
  0.6 74.4 %shard_map.68 = (f32[2,64,1728]{2,1,0:T(8,128)S(1)}, f32[2,64,1728]{2,1,0:T(8,128)S(1)}) custom-call(bf16[6,64,384]{2,1,0:T(8,128)(2,1)} %bitcast.6, bf16[6,64,384]{2,1,0:T(8,128)(2,1)} %bitcast.7, f32[2,64,1728]{2,1,0:T(8,128)} %w_hbm.1, f32[2,64,1728]{2,1,0:T(8,128)} %noise_hbm.1), custom_call_target="tpu_custom_call" | custom-call | tf_op jit(solution)/shard_map/pallas_call | solution.py:488
  75.0 0.0 copy-done
  75.0 1.4 %multiply_subtract_fusion = (f32[2,64,1728]{2,1,0:T(8,128)}, f32[2,64,1728]{2,1,0:T(8,128)}) fusion(f32[2,64,1728]{2,1,0:T(8,128)S(1)} %get-tuple-element.5, f32[2,64,1728]{2,1,0:T(8,128)S(1)} %get-tuple-element.4, f32[2,64,1728]{2,1,0:T(8,128)S(1)} %copy-done), kind=kLoop, calls=%fused_computation | loop fusion | flops 663552 | bytes 4423680 | tf_op jit(solution)/shard_map/sub | solution.py:534
Async XLA Ops:
  0.6 74.4 %copy-start = (f32[2,64,1728]{2,1,0:T(8,128)S(1)}, f32[2,64,1728]{2,1,0:T(8,128)}, u32[]{:S(2)}) copy-start(f32[2,64,1728]{2,1,0:T(8,128)} %param.8) | copy-start | bytes 2654212

commit v4 on v3

--- a/solution.py
+++ b/solution.py
@@ -46,7 +46,7 @@
     feat_hbm, cot_hbm, w_hbm, noise_hbm, out_ref, stepped_ref,
     feat_ref, cot_ref, w_ref, noise_ref,
     cot, masks, kst, kback, im_feat, im_hid, im_cot, parts, normed_one, normed_two, grad,
-    lhs, acc, feat_halo, cot_halo, first_halo, second_halo, rows_out, slots, kg, reduced, scaled, pat_slots, gathered, lengths,
+    lhs, acc, feat_halo, cot_halo, feat_far, im_far, far_parts, outer_first, rows_out, slots, kg, reduced, scaled, pat_slots, gathered, lengths,
     halo_send, halo_recv, row_send, row_recv, red_send, red_recv, pat_send, pat_recv, len_send, len_recv, deep_send, deep_recv, tall_send, tall_recv, core_send, core_recv, load_sem,
 ):
     p = lax.axis_index("pat")
@@ -186,9 +186,11 @@
         taps(feat_ref[j - 1], im_feat, j)
     pl.semaphore_wait(barrier, SLABS - 1 + PATS - 1)
 
-    halos = [halo_copies(0, feat_ref.at[0], feat_ref.at[PLANES - 1], feat_halo), halo_copies(1, cot_ref.at[0], cot_ref.at[PLANES - 1], cot_halo)]
-    for copy in halos[0]:
-        copy.start()
+    halos = [halo_copies(0, feat_ref.at[0], feat_ref.at[PLANES - 1], feat_halo), halo_copies(1, cot_ref.at[0], cot_ref.at[PLANES - 1], cot_halo),
+        halo_copies(2, feat_ref.at[1:3], feat_ref.at[3:5], feat_far)]
+    for pair in (halos[0], halos[2]):
+        for copy in pair:
+            copy.start()
     multiply(kst[0], im_feat, 1, PLANES)
     for copy in halos[0]:
         copy.wait_recv()
@@ -199,20 +201,15 @@
             kst[0, a * C : (a + 1) * C, :], im_feat[0:ROWS, plane(j)], preferred_element_type=F32
         )
 
-    def convolved(target, stage, landing):
+    def convolved(target):
         one = two = jnp.zeros((C, 128), F32)
-        for z in (0, PLANES - 1, 1, 2, 3, 4):
+        for z in range(PLANES):
             value = combined(z)
             target[:, plane(z + 1)] = value
             one, two = one + lane_sum(value), two + lane_sum(value * value)
-            if z == PLANES - 1:
-                pair = halo_copies(stage, target.at[:, plane(1)], target.at[:, plane(PLANES)], landing)
-                for copy in pair:
-                    copy.start()
-        return pair, jnp.sum(one, axis=1, keepdims=True), jnp.sum(two, axis=1, keepdims=True)
-
-    pair, *sums = convolved(normed_one, 2, first_halo)
-    share_pair(0, *sums)
+        return jnp.sum(one, axis=1, keepdims=True), jnp.sum(two, axis=1, keepdims=True)
+
+    share_pair(0, *convolved(normed_one))
 
     for k in range(2):
         for slot in range(OWNERS, SLABS):
@@ -234,15 +231,25 @@
     for im in (im_feat, im_hid):
         im[ROWS:PADDED, :] = jnp.zeros((PADDED - ROWS, WIDE * CELLS), BF16)
 
+    parts[C : 3 * C, plane(0)] = jnp.dot(kst[0, C : 3 * C, :], im_feat[0:ROWS, plane(0)], preferred_element_type=F32)
+    parts[0 : 2 * C, plane(WIDE - 1)] = jnp.dot(
+        kst[0, 0 : 2 * C, :], im_feat[0:ROWS, plane(WIDE - 1)], preferred_element_type=F32
+    )
+    for copy in halos[2]:
+        copy.wait()
+    for i in range(4):
+        taps(feat_far[i // 2, i % 2], im_far, i)
+    far_parts[...] = jnp.dot(kst[0], im_far[...], preferred_element_type=F32)
+    low, mid, high = slice(0, C), slice(C, 2 * C), slice(2 * C, 3 * C)
+    normed_one[:, plane(0)] = far_parts[low, plane(1)] + parts[mid, plane(0)] + parts[high, plane(1)]
+    normed_one[:, plane(WIDE - 1)] = parts[low, plane(6)] + parts[mid, plane(7)] + far_parts[high, plane(2)]
+    outer_first[:, plane(0)] = far_parts[low, plane(0)] + far_parts[mid, plane(1)] + parts[high, plane(0)]
+    outer_first[:, plane(1)] = parts[low, plane(7)] + far_parts[mid, plane(2)] + far_parts[high, plane(3)]
+
     centre_one, squares = pair_total(0)
     for copy in halos[1]:
         copy.start()
     spread_one = lax.rsqrt(squares - centre_one * centre_one + EPS)
-    for copy in pair:
-        copy.wait()
-    normed_one[:, plane(0)] = first_halo[0]
-    normed_one[:, plane(WIDE - 1)] = first_halo[1]
-
     for j in range(WIDE):
         value = (normed_one[:, plane(j)] - centre_one) * spread_one
         normed_one[:, plane(j)] = value
@@ -250,17 +257,17 @@
         if j % 2:
             multiply(kst[1], im_hid, j - 1, 2)
 
-    pair, *sums = convolved(normed_two, 3, second_halo)
-    share_pair(1, *sums)
+    share_pair(1, *convolved(normed_two))
+    for i, j, a in ((0, 0, low), (1, WIDE - 1, high)):
+        value = (outer_first[:, plane(i)] - centre_one) * spread_one
+        taps((value * sigmoid(value) * kept(j)).astype(BF16), im_far, i)
+        far_parts[a, plane(i)] = jnp.dot(kst[1, a, :], im_far[:, plane(i)], preferred_element_type=F32)
+    normed_two[:, plane(0)] = far_parts[low, plane(0)] + parts[mid, plane(0)] + parts[high, plane(1)]
+    normed_two[:, plane(WIDE - 1)] = parts[low, plane(6)] + parts[mid, plane(7)] + far_parts[high, plane(1)]
     centre_two, squares = pair_total(1)
     spread_two = lax.rsqrt(squares - centre_two * centre_two + EPS)
     for copy in halos[1]:
         copy.wait()
-    for copy in pair:
-        copy.wait()
-    normed_two[:, plane(0)] = second_halo[0]
-    normed_two[:, plane(WIDE - 1)] = second_halo[1]
-
     def slope(v):
         h = sigmoid(v)
         return h * (1.0 + v * (1.0 - h))
@@ -510,8 +517,10 @@
             vmem((3 * C, PADDED), F32),
             vmem((2, C, CELLS), BF16),
             vmem((2, C, CELLS), BF16),
-            vmem((2, C, CELLS), F32),
-            vmem((2, C, CELLS), F32),
+            vmem((2, 2, C, CELLS), BF16),
+            vmem((ROWS, 4 * CELLS), BF16),
+            vmem((3 * C, 4 * CELLS), F32),
+            vmem((C, 2 * CELLS), F32),
             vmem((5, 1, 128), F32),
             vmem((5, SLABS, 1, 128), F32),
             vmem((2, OWNERS) + BLOCK, BF16),
@@ -520,7 +529,7 @@
             vmem((PATS,) + BLOCK, F32),
             vmem((2, SLABS) + BLOCK, BF16),
             vmem((PATS, 1, 128), F32),
-            dma((4, 2)), dma((4, 2)), dma((5,)), dma((5,)), dma((2,)), dma((2,)), dma, dma, dma, dma, dma((DEEP,)), dma((DEEP,)), dma((TALL,)), dma((TALL,)), dma((TALL,)), dma((TALL,)), dma((4,)),
+            dma((3, 2)), dma((3, 2)), dma((5,)), dma((5,)), dma((2,)), dma((2,)), dma, dma, dma, dma, dma((DEEP,)), dma((DEEP,)), dma((TALL,)), dma((TALL,)), dma((TALL,)), dma((TALL,)), dma((4,)),
         ],
         compiler_params=pltpu.CompilerParams(
             collective_id=0, has_side_effects=True, vmem_limit_bytes=32 * 1024 * 1024

time: 76.5 us -> 75 us (0.980)
  Pallas kernels: 74.4 us -> 72.9 us
    pallas_call x1, Pallas kernels: 74.4 us -> 72.9 us  [clipped_gradients(): pl.pallas_call(kernel, out_shape=[jax.ShapeDtypeStruct((2, C, 3 * ROWS),...]
where the time goes in v4:
time: 75 us; the launch traced here: 74.9 us
  Pallas kernels  72.9 us (97%)
  other arithmetic  1.4 us (2%)
    pallas_call x1, Pallas kernels, clipped_gradients(): pl.pallas_call(kernel, out_shape=[jax.ShapeDtypeStruct((2, C, 3 * ROWS),...  72.9 us

profile of v4, /device:TPU:1, one launch (start us, length us, event | category | flops | bytes accessed | tf_op | source)
XLA Modules:
  0.0 74.9 jit_solution(15888939207198256608)
XLA Ops:
  0.6 0.0 copy-start
  0.6 72.9 %shard_map.68 = (f32[2,64,1728]{2,1,0:T(8,128)S(1)}, f32[2,64,1728]{2,1,0:T(8,128)S(1)}) custom-call(bf16[6,64,384]{2,1,0:T(8,128)(2,1)} %bitcast.6, bf16[6,64,384]{2,1,0:T(8,128)(2,1)} %bitcast.7, f32[2,64,1728]{2,1,0:T(8,128)} %w_hbm.1, f32[2,64,1728]{2,1,0:T(8,128)} %noise_hbm.1), custom_call_target="tpu_custom_call" | custom-call | tf_op jit(solution)/shard_map/pallas_call | solution.py:495
  73.5 0.0 copy-done
  73.5 1.4 %multiply_subtract_fusion = (f32[2,64,1728]{2,1,0:T(8,128)}, f32[2,64,1728]{2,1,0:T(8,128)}) fusion(f32[2,64,1728]{2,1,0:T(8,128)S(1)} %get-tuple-element.5, f32[2,64,1728]{2,1,0:T(8,128)S(1)} %get-tuple-element.4, f32[2,64,1728]{2,1,0:T(8,128)S(1)} %copy-done), kind=kLoop, calls=%fused_computation | loop fusion | flops 663552 | bytes 4423680 | tf_op jit(solution)/shard_map/sub | solution.py:543
Async XLA Ops:
  0.6 72.9 %copy-start = (f32[2,64,1728]{2,1,0:T(8,128)S(1)}, f32[2,64,1728]{2,1,0:T(8,128)}, u32[]{:S(2)}) copy-start(f32[2,64,1728]{2,1,0:T(8,128)} %param.8) | copy-start | bytes 2654212

commit v5 on v4

--- a/solution.py
+++ b/solution.py
@@ -46,7 +46,7 @@
     feat_hbm, cot_hbm, w_hbm, noise_hbm, out_ref, stepped_ref,
     feat_ref, cot_ref, w_ref, noise_ref,
     cot, masks, kst, kback, im_feat, im_hid, im_cot, parts, normed_one, normed_two, grad,
-    lhs, acc, feat_halo, cot_halo, feat_far, im_far, far_parts, outer_first, rows_out, slots, kg, reduced, scaled, pat_slots, gathered, lengths,
+    lhs, acc, feat_halo, cot_halo, feat_far, im_far, far_parts, outer_first, slope_one, rows_out, slots, kg, reduced, scaled, pat_slots, gathered, lengths,
     halo_send, halo_recv, row_send, row_recv, red_send, red_recv, pat_send, pat_recv, len_send, len_recv, deep_send, deep_recv, tall_send, tall_recv, core_send, core_recv, load_sem,
 ):
     p = lax.axis_index("pat")
@@ -139,8 +139,8 @@
         return jnp.sum(slots[r], axis=0)
 
     def share_pair(r, one, two):
-        column = jnp.concatenate([one, two], axis=0)
-        share_row(r, jnp.sum(jnp.where(eye(), column, 0.0), axis=0, keepdims=True))
+        lanes = jnp.transpose(jnp.concatenate([one, two], axis=0))
+        share_row(r, jnp.sum(lanes, axis=0, keepdims=True))
 
     def pair_total(r):
         row = row_total(r) * (1.0 / COUNT)
@@ -207,7 +207,7 @@
             value = combined(z)
             target[:, plane(z + 1)] = value
             one, two = one + lane_sum(value), two + lane_sum(value * value)
-        return jnp.sum(one, axis=1, keepdims=True), jnp.sum(two, axis=1, keepdims=True)
+        return one, two
 
     share_pair(0, *convolved(normed_one))
 
@@ -257,6 +257,10 @@
         if j % 2:
             multiply(kst[1], im_hid, j - 1, 2)
 
+    def slope(v):
+        h = sigmoid(v)
+        return h * (1.0 + v * (1.0 - h))
+
     share_pair(1, *convolved(normed_two))
     for i, j, a in ((0, 0, low), (1, WIDE - 1, high)):
         value = (outer_first[:, plane(i)] - centre_one) * spread_one
@@ -268,10 +272,6 @@
     spread_two = lax.rsqrt(squares - centre_two * centre_two + EPS)
     for copy in halos[1]:
         copy.wait()
-    def slope(v):
-        h = sigmoid(v)
-        return h * (1.0 + v * (1.0 - h))
-
     def second_gradient(j, carry, upstream=None):
         value = (normed_two[:, plane(j)] - centre_two) * spread_two
         normed_two[:, plane(j)] = value
@@ -285,9 +285,11 @@
     for j in range(1, WIDE - 1):
         carry = second_gradient(j, carry)
     one, two = carry
-    share_pair(2, jnp.sum(one, axis=1, keepdims=True), jnp.sum(two, axis=1, keepdims=True))
+    share_pair(2, one, two)
     second_gradient(0, (zero, zero), cot_halo[0])
     second_gradient(WIDE - 1, (zero, zero), cot_halo[1])
+    for j in range(1, WIDE - 1):
+        slope_one[:, plane(j)] = slope(normed_one[:, plane(j)])
     mean_two, cross_two = pair_total(2)
 
     for j in range(WIDE):
@@ -300,7 +302,7 @@
 
     def first_gradient(j, carry):
         value = normed_one[:, plane(j + 1)]
-        g = combined(j) * slope(value)
+        g = combined(j) * slope_one[:, plane(j + 1)]
         grad[:, plane(j + 1)] = g
         return carry[0] + lane_sum(g), carry[1] + lane_sum(g * value)
 
@@ -308,7 +310,7 @@
     for j in range(PLANES):
         carry = first_gradient(j, carry)
     one, two = carry
-    share_pair(3, jnp.sum(one, axis=1, keepdims=True), jnp.sum(two, axis=1, keepdims=True))
+    share_pair(3, one, two)
 
     def kernel_gradient(k, im):
         def send(first, count):
@@ -521,6 +523,7 @@
             vmem((ROWS, 4 * CELLS), BF16),
             vmem((3 * C, 4 * CELLS), F32),
             vmem((C, 2 * CELLS), F32),
+            vmem((C, wide), F32),
             vmem((5, 1, 128), F32),
             vmem((5, SLABS, 1, 128), F32),
             vmem((2, OWNERS) + BLOCK, BF16),

time: 75 us -> 74.8 us (level)
  no operation moved by 1% of the time
where the time goes in v5:
time: 74.8 us; the launch traced here: 74.7 us
  Pallas kernels  72.6 us (97%)
  other arithmetic  1.4 us (2%)
    pallas_call x1, Pallas kernels, clipped_gradients(): pl.pallas_call(kernel, out_shape=[jax.ShapeDtypeStruct((2, C, 3 * ROWS),...  72.6 us

profile of v5, /device:TPU:1, one launch (start us, length us, event | category | flops | bytes accessed | tf_op | source)
XLA Modules:
  0.0 74.7 jit_solution(170871589429387021)
XLA Ops:
  0.6 0.0 copy-start
  0.6 72.6 %shard_map.68 = (f32[2,64,1728]{2,1,0:T(8,128)S(1)}, f32[2,64,1728]{2,1,0:T(8,128)S(1)}) custom-call(bf16[6,64,384]{2,1,0:T(8,128)(2,1)} %bitcast.6, bf16[6,64,384]{2,1,0:T(8,128)(2,1)} %bitcast.7, f32[2,64,1728]{2,1,0:T(8,128)} %w_hbm.1, f32[2,64,1728]{2,1,0:T(8,128)} %noise_hbm.1), custom_call_target="tpu_custom_call" | custom-call | tf_op jit(solution)/shard_map/pallas_call | solution.py:497
  73.3 0.0 copy-done
  73.3 1.4 %multiply_subtract_fusion = (f32[2,64,1728]{2,1,0:T(8,128)}, f32[2,64,1728]{2,1,0:T(8,128)}) fusion(f32[2,64,1728]{2,1,0:T(8,128)S(1)} %get-tuple-element.5, f32[2,64,1728]{2,1,0:T(8,128)S(1)} %get-tuple-element.4, f32[2,64,1728]{2,1,0:T(8,128)S(1)} %copy-done), kind=kLoop, calls=%fused_computation | loop fusion | flops 663552 | bytes 4423680 | tf_op jit(solution)/shard_map/sub | solution.py:546
Async XLA Ops:
  0.6 72.6 %copy-start = (f32[2,64,1728]{2,1,0:T(8,128)S(1)}, f32[2,64,1728]{2,1,0:T(8,128)}, u32[]{:S(2)}) copy-start(f32[2,64,1728]{2,1,0:T(8,128)} %param.8) | copy-start | bytes 2654212

commit v6 on v5

--- a/solution.py
+++ b/solution.py
@@ -116,11 +116,6 @@
             return 1.0
         return jnp.where(s == (0 if j == 0 else SLABS - 1), 0.0, 1.0).astype(F32)
 
-    def eye():
-        i = lax.broadcasted_iota(jnp.int32, (128, 128), 0)
-        j = lax.broadcasted_iota(jnp.int32, (128, 128), 1)
-        return i == j
-
     def share_row(r, row):
         rows_out[r] = row
 
@@ -144,7 +139,7 @@
 
     def pair_total(r):
         row = row_total(r) * (1.0 / COUNT)
-        column = jnp.sum(jnp.where(eye(), row, 0.0), axis=1, keepdims=True)
+        column = jnp.transpose(jnp.broadcast_to(row, (128, 128)))[:, :1]
         return column[:C], column[C:]
 
     def taps(values, im, j):

time: 74.8 us -> 74.9 us (level)
  no operation moved by 1% of the time
where the time goes in v6:
time: 74.9 us; the launch traced here: 74.8 us
  Pallas kernels  72.8 us (97%)
  other arithmetic  1.4 us (2%)
    pallas_call x1, Pallas kernels, clipped_gradients(): pl.pallas_call(kernel, out_shape=[jax.ShapeDtypeStruct((2, C, 3 * ROWS),...  72.8 us

profile of v6, /device:TPU:1, one launch (start us, length us, event | category | flops | bytes accessed | tf_op | source)
XLA Modules:
  0.0 74.8 jit_solution(869069036543892289)
XLA Ops:
  0.6 0.0 copy-start
  0.6 72.8 %shard_map.68 = (f32[2,64,1728]{2,1,0:T(8,128)S(1)}, f32[2,64,1728]{2,1,0:T(8,128)S(1)}) custom-call(bf16[6,64,384]{2,1,0:T(8,128)(2,1)} %bitcast.6, bf16[6,64,384]{2,1,0:T(8,128)(2,1)} %bitcast.7, f32[2,64,1728]{2,1,0:T(8,128)} %w_hbm.1, f32[2,64,1728]{2,1,0:T(8,128)} %noise_hbm.1), custom_call_target="tpu_custom_call" | custom-call | tf_op jit(solution)/shard_map/pallas_call | solution.py:492
  73.4 0.0 copy-done
  73.4 1.4 %multiply_subtract_fusion = (f32[2,64,1728]{2,1,0:T(8,128)}, f32[2,64,1728]{2,1,0:T(8,128)}) fusion(f32[2,64,1728]{2,1,0:T(8,128)S(1)} %get-tuple-element.5, f32[2,64,1728]{2,1,0:T(8,128)S(1)} %get-tuple-element.4, f32[2,64,1728]{2,1,0:T(8,128)S(1)} %copy-done), kind=kLoop, calls=%fused_computation | loop fusion | flops 663552 | bytes 4423680 | tf_op jit(solution)/shard_map/sub | solution.py:541
Async XLA Ops:
  0.6 72.8 %copy-start = (f32[2,64,1728]{2,1,0:T(8,128)S(1)}, f32[2,64,1728]{2,1,0:T(8,128)}, u32[]{:S(2)}) copy-start(f32[2,64,1728]{2,1,0:T(8,128)} %param.8) | copy-start | bytes 2654212
